TPU v7x, 32 devices: a whole 2x2x4 slice. The times are simulated.
32 devices in a mesh: grp: 2 (over x), ep: 8 (over z, y), tp: 2 (over core).
Axes of the slice: x: 2, y: 2, z: 4, core: 2. Of those that a mesh axis runs over, the one named last changes fastest.
Arguments:
- query_rows: bfloat16 [1024, 1152], P(('grp', 'ep'), 'tp'), parts along dimension 0, may hold values from -160 to 160, as said below
- key_rows: bfloat16 [1024, 1152], P(('grp', 'ep'), 'tp'), parts along dimension 0, may hold values from -4 to 4
- value_rows: bfloat16 [1024, 1152], P(('grp', 'ep'), 'tp'), parts along dimension 0, may hold values from -6 to 6
- merger_weight: bfloat16 [4, 1152, 4096], P(None, 'tp', 'ep'), may hold values from -0.09375 to 0.09375
- visual_counts: int32 [16], P('grp'), parts along dimension 0, may hold values from 1 to 32, 128 in all
- text_rows: bfloat16 [512, 4096], P(('grp', 'ep')), parts along dimension 0, may hold values from -6 to 6
- norm_gain: float32 [4096], replicated, may hold values from 0.1 to 1.9
- route_ids: int32 [1024, 8], P(('grp', 'ep')), parts along dimension 0, may hold values from 0 to 31, all different within a row; in each aligned block of 32 rows (0 to 31, 32 to 63, ...) at most 16 rows name the same one
- route_gates: float32 [1024, 8], P(('grp', 'ep')), parts along dimension 0, may hold values from 0.03 to 0.4
- gate_weight: bfloat16 [32, 4096, 768], P('ep', None, 'tp'), may hold values from -0.09375 to 0.09375
- up_weight: bfloat16 [32, 4096, 768], P('ep', None, 'tp'), may hold values from -0.09375 to 0.09375
- down_weight: bfloat16 [32, 768, 4096], P('ep', 'tp'), may hold values from -0.21875 to 0.21875
Outputs:
- moe_out: bfloat16 [1024, 4096], P(('grp', 'ep')), parts along dimension 0
There are 2 independent parts, one for each index of `grp`. A program takes and returns all parts, laid end to end along the dimension named above; an argument that names none is the same for every part. Nothing has to cross between parts.
Inputs may be any that keep to these rules, and one draw needn't show every extreme that they name: `query_rows`: rows of the image in order. `visual_counts`: visual rows for each language owner in order of owners; they sum to 128 and the largest is exactly 32. `route_ids`: each row names 8 different experts; in each aligned block of 32 rows no expert is named by more than 16 rows; ids of visual slots at or past their owner's count are not used.
All inputs are finite; a program needn't handle non-finite values.
Results may differ from a plain program's by a relative error of at most 0.0065.
Values may be sent and summed in bfloat16 or wider, within the bound.
A program may use at most 128 MiB of HBM per device.

v0:
```python
import jax
import jax.numpy as jnp
from jax import lax
from jax.sharding import PartitionSpec as P

HEAD_DIM = 72
MERGE = 4


def share_slots(share_ids, share_live, expert_count, capacity):
    flat_ids = share_ids.reshape(-1)
    flat_live = jnp.repeat(share_live, share_ids.shape[1])
    experts_iota = jnp.arange(expert_count, dtype=jnp.int32)
    onehot_table = ((flat_ids[:, None] == experts_iota[None, :]) & flat_live[:, None]).astype(
        jnp.int32
    )
    before = jnp.cumsum(onehot_table, axis=0) - onehot_table
    rank_in_expert = jnp.sum(before * onehot_table, axis=1)
    slot_ids = jnp.where(flat_live, flat_ids * capacity + rank_in_expert, -1)
    return slot_ids.reshape(share_ids.shape)


def pack_share(slot_ids, block_rows, expert_count, capacity):
    places = jnp.arange(expert_count * capacity, dtype=jnp.int32)
    picker = jnp.any(slot_ids[None, :, :] == places[:, None, None], axis=2).astype(jnp.bfloat16)
    packed = jnp.dot(picker, block_rows, preferred_element_type=jnp.float32).astype(jnp.bfloat16)
    return packed.reshape(expert_count, capacity, block_rows.shape[1])


def run_experts(grouped, gate_part, up_part, down_part):
    gate_value = jnp.einsum(
        "nlcd,ldf->nlcf", grouped, gate_part, preferred_element_type=jnp.float32
    )
    up_value = jnp.einsum("nlcd,ldf->nlcf", grouped, up_part, preferred_element_type=jnp.float32)
    hidden = (jax.nn.silu(gate_value) * up_value).astype(jnp.bfloat16)
    return jnp.einsum("nlcf,lfd->nlcd", hidden, down_part, preferred_element_type=jnp.float32)


def body(
    query_rows,
    key_rows,
    value_rows,
    merger_weight,
    visual_counts,
    text_rows,
    norm_gain,
    route_ids,
    route_gates,
    gate_weight,
    up_weight,
    down_weight,
):
    owner_count = lax.axis_size("ep")
    core_count = lax.axis_size("tp")
    owner_index = lax.axis_index("ep")
    core_index = lax.axis_index("tp")
    patch_count = query_rows.shape[0]
    local_heads = query_rows.shape[1] // HEAD_DIM
    score_scale = HEAD_DIM ** (-0.5)
    queries = query_rows.reshape(patch_count, local_heads, HEAD_DIM)
    running_max = jnp.full((patch_count, local_heads), -1e30, jnp.float32)
    key_segment = lax.all_gather(key_rows, "ep", axis=0, tiled=True)
    value_segment = lax.all_gather(value_rows, "ep", axis=0, tiled=True)
    key_count = key_segment.shape[0]
    key_heads = key_segment.reshape(key_count, local_heads, HEAD_DIM)
    value_heads = value_segment.reshape(key_count, local_heads, HEAD_DIM)
    scores = (
        jnp.einsum("qhd,khd->qhk", queries, key_heads, preferred_element_type=jnp.float32)
        * score_scale
    )
    new_max = jnp.maximum(running_max, jnp.max(scores, axis=2))
    weights = jnp.exp(scores - new_max[:, :, None])
    running_sum = jnp.sum(weights, axis=2)
    running_acc = jnp.einsum(
        "qhk,khd->qhd",
        weights.astype(jnp.bfloat16),
        value_heads,
        preferred_element_type=jnp.float32,
    )
    attended = (
        (running_acc / running_sum[:, :, None])
        .astype(jnp.bfloat16)
        .reshape(patch_count, local_heads * HEAD_DIM)
    )
    merged_local = attended.reshape(patch_count // MERGE, MERGE * attended.shape[1])
    merger_local = merger_weight.reshape(-1, merger_weight.shape[2])
    partial_visual = jnp.dot(
        lax.all_gather(merged_local, "ep", axis=0, tiled=True),
        merger_local,
        preferred_element_type=jnp.float32,
    )
    visual_total = partial_visual.shape[0]
    slot_count = 2 * patch_count // MERGE
    offsets = jnp.cumsum(visual_counts) - visual_counts
    positions = jnp.arange(slot_count, dtype=jnp.int32)
    filled = positions[None, :] < visual_counts[:, None]
    sources = jnp.clip(offsets[:, None] + positions[None, :], 0, visual_total - 1)
    outgoing = jnp.where(filled[:, :, None], partial_visual[sources], jnp.zeros((), jnp.float32))
    arrived = lax.all_to_all(
        outgoing.astype(jnp.bfloat16), "ep", split_axis=0, concat_axis=2, tiled=True
    ).astype(outgoing.dtype)
    visual_rows = lax.psum(arrived.reshape(slot_count, -1).astype(jnp.bfloat16), "tp")
    my_count = visual_counts[owner_index]
    all_rows = jnp.concatenate([text_rows, visual_rows], axis=0)
    live_rows = jnp.concatenate([jnp.ones((text_rows.shape[0],), jnp.bool_), positions < my_count])
    values = all_rows.astype(jnp.float32)
    normed = (
        values * lax.rsqrt(jnp.mean(values * values, axis=1, keepdims=True) + 1e-06) * norm_gain
    ).astype(jnp.bfloat16)
    share_size = all_rows.shape[0] // core_count
    local_experts = gate_weight.shape[0]
    expert_count = local_experts * owner_count
    top_count = route_ids.shape[1]
    capacity = 2 * share_size * top_count // expert_count
    model_width = normed.shape[1]

    def share_plan(share_index):
        ids_part = lax.dynamic_slice_in_dim(route_ids, share_index * share_size, share_size, 0)
        live_part = lax.dynamic_slice_in_dim(live_rows, share_index * share_size, share_size, 0)
        return share_slots(ids_part, live_part, expert_count, capacity)

    share_plans = [share_plan(share_index) for share_index in range(core_count)]
    packed = jnp.stack(
        [
            pack_share(
                share_plans[share_index],
                normed[share_index * share_size : (share_index + 1) * share_size],
                expert_count,
                capacity,
            )
            for share_index in range(core_count)
        ]
    )
    received = lax.all_to_all(packed, "ep", split_axis=1, concat_axis=1, tiled=True)
    own_slots = jnp.stack(share_plans)[core_index]
    flat_in = received.reshape(-1, received.shape[3])
    block_count = flat_in.shape[0] // core_count
    grouped = flat_in.reshape(
        lax.axis_size("tp") * block_count // (local_experts * capacity),
        local_experts,
        capacity,
        flat_in.shape[1],
    )
    output = run_experts(grouped, gate_weight, up_weight, down_weight)
    expert_out = lax.psum_scatter(
        output.reshape(lax.axis_size("tp") * block_count, flat_in.shape[1]).astype(jnp.bfloat16),
        "tp",
        scatter_dimension=0,
        tiled=True,
    )
    returned = lax.all_to_all(
        expert_out.reshape(owner_count, -1, model_width),
        "ep",
        split_axis=0,
        concat_axis=0,
        tiled=True,
    ).reshape(-1, model_width)
    gates_part = lax.dynamic_slice_in_dim(route_gates, core_index * share_size, share_size, 0)
    active = own_slots >= 0
    picked = returned[jnp.maximum(own_slots, 0)]
    weight_grid = jnp.where(active, gates_part, jnp.zeros((), jnp.float32))
    combined = jnp.sum(weight_grid[:, :, None] * picked.astype(jnp.float32), axis=1)
    residual = lax.dynamic_slice_in_dim(values, core_index * share_size, share_size, 0)
    share_out = (residual + combined).astype(jnp.bfloat16)
    return lax.all_gather(share_out, "tp", axis=0, tiled=True)


def solution(mesh):
    return jax.shard_map(
        body,
        mesh=mesh,
        in_specs=(
            P(("grp", "ep"), "tp"),
            P(("grp", "ep"), "tp"),
            P(("grp", "ep"), "tp"),
            P(None, "tp", "ep"),
            P("grp"),
            P(("grp", "ep"), None),
            P(),
            P(("grp", "ep"), None),
            P(("grp", "ep"), None),
            P("ep", None, "tp"),
            P("ep", None, "tp"),
            P("ep", "tp", None),
        ),
        out_specs=P(("grp", "ep"), None),
        check_vma=False,
    )
```

profile of v0, /device:TPU:17, one launch (start us, length us, event | category | flops | bytes accessed | tf_op | source)
XLA Modules:
  0.0 528.8 jit_solution(11199886660944515788)
XLA Ops:
  6.5 22.4 %all_gather.12 = bf16[512,576]{1,0:T(8,128)(2,1)S(1)} all-gather(bf16[64,576]{1,0:T(8,128)(2,1)} %param.13), channel_id=1, replica_groups=mesh['grp'=2,'ep'=8,'tp'=2] {'ep'}, dimensions={0}, use_global_device_ids=true | all-gather | bytes 663552 | tf_op jit(solution)/shard_map/all_gather | solution.py:62
  28.9 1.0 copy.51
  30.0 1.0 reshape.207
  31.0 1.4 fusion.49
  32.5 28.8 %all_gather.13 = bf16[512,576]{1,0:T(8,128)(2,1)} all-gather(bf16[64,576]{1,0:T(8,128)(2,1)} %param.14), channel_id=1, replica_groups=mesh['grp'=2,'ep'=8,'tp'=2] {'ep'}, dimensions={0}, use_global_device_ids=true | all-gather | bytes 663552 | tf_op jit(solution)/shard_map/all_gather | solution.py:63
  61.3 2.1 copy.53
  63.4 0.4 fusion.26
  63.8 1.4 fusion.25
  65.2 0.1 copy.54
  65.3 0.2 reshape_reshape.6
  65.5 26.2 %all_gather.14 = bf16[128,2304]{1,0:T(8,128)(2,1)S(1)} all-gather(bf16[16,2304]{1,0:T(8,128)(2,1)S(1)} %reshape_reshape.6), channel_id=1, replica_groups=mesh['grp'=2,'ep'=8,'tp'=2] {'ep'}, dimensions={0}, use_global_device_ids=true | all-gather | bytes 663552 | tf_op jit(solution)/shard_map/all_gather | solution.py:88
  91.8 0.7 iota_compare_fusion.6
  92.5 0.8 reduce-window.24
  93.3 0.7 bitcast_subtract_fusion
  94.0 0.1 compare_select_fusion
  94.1 0.1 reshape.218
  94.2 0.5 fusion.50
  94.6 1.2 gather_fusion
  95.8 0.8 select_convert_fusion
  96.6 7.8 %all-to-all-start = ((bf16[8,32,512]{2,1,0:T(8,128)(2,1)}), bf16[8,32,512]{2,1,0:T(8,128)(2,1)S(1)}, u32[]{:S(2)}, u32[]{:S(2)}) async-start(bf16[8,32,512]{2,1,0:T(8,128)(2,1)} %select_convert_fusion), calls=%async_computation | async-start | bytes 524288 | tf_op jit(solution)/shard_map/all_to_all | solution.py:99
  104.4 0.7 dynamic_slice.20
  105.0 0.7 add_compare_fusion
  105.7 0.7 iota_compare_fusion.7
  106.5 0.1 copy.74
  106.6 0.1 eq.88
  106.7 0.1 eq.84
  106.9 0.1 broadcast_in_dim.52
  107.0 0.6 reduce-window.32
  107.6 0.2 slice_reduce_fusion
  107.9 0.1 and.18
  108.0 0.1 copy.73
  108.1 0.1 eq.80
  108.2 0.1 fusion.38
  108.3 0.1 eq.76
  108.3 0.1 reduce_sum.53
  108.4 0.6 reduce-window.30
  109.0 0.2 slice_reduce_fusion.1
  109.2 0.1 fusion.41
  109.4 0.1 reduce_sum.51
  109.4 0.1 add_select_fusion
  109.5 0.7 copy.77
  110.3 0.2 fusion.32
  110.6 0.2 fusion.31
  110.8 38.5 %all-reduce.2.cloned.1.call-done = bf16[32,4096]{1,0:T(8,128)(2,1)} async-done(((bf16[32,4096]{1,0:T(8,128)(2,1)}), bf16[32,4096]{1,0:T(8,128)(2,1)}) %all-reduce.2.cloned.1.call-update) | async-done | bytes 262160 | tf_op jit(solution)/shard_map/psum | solution.py:102
  149.3 1.2 multiply_reduce_fusion
  150.4 1.1 multiply_convert_fusion
  151.6 1.3 convolution_convert_fusion
  152.9 3.3 convolution_convert_fusion.1
  156.2 6.2 %pad_maximum_fusion = bf16[2,32,16,4096]{3,2,0,1:T(8,128)(2,1)} fusion(bf16[1,32,16,4096]{3,2,0,1:T(8,128)(2,1)S(1)} %bitcast.133, bf16[1,32,16,4096]{3,2,0,1:T(8,128)(2,1)} %bitcast.134), kind=kLoop, calls=%fused_computation.8 | loop fusion | flops 4194304 | bytes 16777216 | tf_op jit(solution)/shard_map/stack | solution.py:123
  162.4 187.5 %all_to_all.28 = bf16[2,32,16,4096]{3,2,0,1:T(8,128)(2,1)} all-to-all(bf16[2,32,16,4096]{3,2,0,1:T(8,128)(2,1)} %pad_maximum_fusion), channel_id=1, replica_groups=mesh['grp'=2,'ep'=8,'tp'=2] {'ep'}, dimensions={1} | all-to-all | bytes 16777216 | tf_op jit(solution)/shard_map/all_to_all | solution.py:134
  349.9 7.7 %copy.65 = bf16[2,32,16,4096]{3,2,1,0:T(8,128)(2,1)} copy(bf16[2,32,16,4096]{3,2,0,1:T(8,128)(2,1)} %all_to_all.28) | data formatting | bytes 16777216 | tf_op jit(solution)/shard_map/all_to_all | solution.py:134
  357.6 10.6 %fusion.4 = f32[4,16,16,384]{3,2,1,0:T(8,128)S(1)} fusion(bf16[4,4096,384]{2,1,0:T(8,128)(2,1)} %param.21, bf16[16,4,16,4096]{3,2,1,0:T(8,128)(2,1)} %bitcast.135), kind=kOutput, calls=%fused_computation.6 | convolution fusion | flops 3221225472 | bytes 22544384 | tf_op jit(solution)/shard_map/nlcd,ldf->nlcf/dot_general | solution.py:31
  368.2 17.2 %convert_bitcast_fusion = bf16[16,4,16,4096]{3,2,0,1:T(8,128)(2,1)} fusion(bf16[4,384,4096]{2,1,0:T(8,128)(2,1)} %param.23, f32[4,16,16,384]{3,2,1,0:T(8,128)S(1)} %fusion.4, bf16[4,4096,384]{2,1,0:T(8,128)(2,1)} %param.22, bf16[16,4,16,4096]{3,2,1,0:T(8,128)(2,1)} %bitcast.136), kind=kOutput, calls=%fused_computation.9 | convolution fusion | flops 6449004544 | bytes 43515904 | tf_op jit(solution)/shard_map/nlcf,lfd->nlcd/dot_general | solution.py:36
  385.4 7.7 %copy.68 = bf16[16,4,16,4096]{3,2,1,0:T(8,128)(2,1)} copy(bf16[16,4,16,4096]{3,2,0,1:T(8,128)(2,1)} %convert_bitcast_fusion) | data formatting | bytes 16777216 | tf_op jit(solution)/shard_map/convert_element_type | solution.py:146
  393.1 18.2 %reduce-scatter.2.cloned.1.call-done = bf16[512,4096]{1,0:T(8,128)(2,1)} async-done(((bf16[1024,4096]{1,0:T(8,128)(2,1)}), bf16[512,4096]{1,0:T(8,128)(2,1)}) %reduce-scatter.2.cloned.1.call-update) | async-done | bytes 4194320 | tf_op jit(solution)/shard_map/reduce_scatter | solution.py:145
  411.4 5.5 %all-to-all-start.2 = ((bf16[8,64,4096]{2,1,0:T(8,128)(2,1)}), bf16[8,64,4096]{2,1,0:T(8,128)(2,1)}, u32[]{:S(2)}, u32[]{:S(2)}) async-start(bf16[8,64,4096]{2,1,0:T(8,128)(2,1)} %bitcast.137), calls=%async_computation.3 | async-start | bytes 8388608 | tf_op jit(solution)/shard_map/all_to_all | solution.py:151
  417.0 0.1 copy.69
  417.1 0.1 reshape.226
  417.3 0.1 copy.62
  417.4 89.2 %all-to-all-done.2 = bf16[8,64,4096]{2,1,0:T(8,128)(2,1)} async-done(((bf16[8,64,4096]{2,1,0:T(8,128)(2,1)}), bf16[8,64,4096]{2,1,0:T(8,128)(2,1)}, u32[]{:S(2)}, u32[]{:S(2)}) %all-to-all-start.2) | async-done | bytes 4194336 | tf_op jit(solution)/shard_map/all_to_all | solution.py:151
  506.6 8.1 %gather_fusion.1 = bf16[256,4096]{1,0:T(8,128)(2,1)} fusion(bf16[512,4096]{1,0:T(8,128)(2,1)} %bitcast.32, s32[1024]{0:T(1024)S(1)} %pad_clamp_fusion), kind=kCustom, calls=%fused_computation.1 | custom fusion | bytes 4195328 | tf_op jit(solution)/shard_map/gather | solution.py:160
  514.7 3.2 fusion.10
  518.0 3.2 all_gather.15
  521.2 0.8 copy.95
  (43 shorter events, 0.8 us)
Async XLA Ops:
  6.5 87.6 %copy-start = (bf16[4,576,512]{2,1,0:T(8,128)(2,1)S(1)}, bf16[4,576,512]{2,1,0:T(8,128)(2,1)}, u32[]{:S(2)}) copy-start(bf16[4,576,512]{2,1,0:T(8,128)(2,1)} %param.15) | copy-start | bytes 7077892
  31.0 119.4 %copy-start.5 = (f32[4096]{0:T(1024)S(1)}, f32[4096]{0:T(1024)}, u32[]{:S(2)}) copy-start(f32[4096]{0:T(1024)} %param.18) | copy-start | bytes 49156
  32.4 71.9 %copy-start.8 = (s32[8]{0:T(128)S(1)}, s32[8]{0:T(128)}, u32[]{:S(2)}) copy-start(s32[8]{0:T(128)} %param.16) | copy-start | bytes 100
  32.5 74.0 %copy-start.6 = (s32[64,8]{0,1:T(8,128)S(1)}, s32[64,8]{0,1:T(8,128)}, u32[]{:S(2)}) copy-start(s32[64,8]{0,1:T(8,128)} %param.19) | copy-start | bytes 6148
  65.2 84.0 %copy-start.2 = (bf16[32,4096]{1,0:T(8,128)(2,1)S(1)}, bf16[32,4096]{1,0:T(8,128)(2,1)}, u32[]{:S(2)}) copy-start(bf16[32,4096]{1,0:T(8,128)(2,1)} %param.17) | copy-start | bytes 786436
  96.6 12.9 %all-to-all-start = ((bf16[8,32,512]{2,1,0:T(8,128)(2,1)}), bf16[8,32,512]{2,1,0:T(8,128)(2,1)S(1)}, u32[]{:S(2)}, u32[]{:S(2)}) async-start(bf16[8,32,512]{2,1,0:T(8,128)(2,1)} %select_convert_fusion), calls=%async_computation | async-start | bytes 524288 | tf_op jit(solution)/shard_map/all_to_all | solution.py:99
  104.4 44.9 %all-reduce.2.cloned.1.call-start = ((), (), s32[]{:S(2)}) async-start(), calls=%async_computation.4 | async-start | bytes 524288 | tf_op jit(solution)/shard_map/psum | solution.py:102
  110.3 301.1 %reduce-scatter.2.cloned.1.call-start = ((), (), s32[]{:S(2)}) async-start(), calls=%async_computation.5 | async-start | bytes 12582912 | tf_op jit(solution)/shard_map/reduce_scatter | solution.py:145
  393.1 24.1 %copy-start.7 = (f32[64,8]{0,1:T(8,128)S(1)}, f32[64,8]{0,1:T(8,128)}, u32[]{:S(2)}) copy-start(f32[64,8]{0,1:T(8,128)} %param.20) | copy-start | bytes 6148
  393.1 24.2 %copy-start.3 = (bf16[32,4096]{1,0:T(8,128)(2,1)S(1)}, bf16[32,4096]{1,0:T(8,128)(2,1)}, u32[]{:S(2)}) copy-start(bf16[32,4096]{1,0:T(8,128)(2,1)} %param.17) | copy-start | bytes 786436
  393.1 24.2 %copy-start.4 = (bf16[32,4096]{1,0:T(8,128)(2,1)S(1)}, bf16[32,4096]{1,0:T(8,128)(2,1)}, u32[]{:S(2)}) copy-start(bf16[32,4096]{1,0:T(8,128)(2,1)} %all-reduce.2.cloned.1.call-done) | copy-start | bytes 786436
  411.4 95.2 %all-to-all-start.2 = ((bf16[8,64,4096]{2,1,0:T(8,128)(2,1)}), bf16[8,64,4096]{2,1,0:T(8,128)(2,1)}, u32[]{:S(2)}, u32[]{:S(2)}) async-start(bf16[8,64,4096]{2,1,0:T(8,128)(2,1)} %bitcast.137), calls=%async_computation.3 | async-start | bytes 8388608 | tf_op jit(solution)/shard_map/all_to_all | solution.py:151
  506.6 15.4 %copy-start.1 = (bf16[4,576,512]{2,1,0:T(8,128)(2,1)S(1)}, bf16[4,576,512]{2,1,0:T(8,128)(2,1)}, u32[]{:S(2)}) copy-start(bf16[4,576,512]{2,1,0:T(8,128)(2,1)} %param.15) | copy-start | bytes 7077892
Sparse Core Ops, SparseCore 0:
  110.4 38.8 all-reduce.1
  393.3 18.0 reduce-scatter.1
where the time goes:
time: 534 us; the launch traced here: 529 us
  blocking collectives  268 us (50%)
  waiting for transfers between devices  146 us (27%)
  matrix products  35.7 us (7%)
  local copies, waits for them, and re-layouts  33.3 us (6%)
  other arithmetic  18.8 us (4%)
  between operations  13.7 us (3%)
  starting transfers between devices  13.3 us (2%)
    all_to_all x1, blocking collectives, body(): lax.all_to_all(packed, 'ep', split_axis=1, concat_axis=1, tiled=True)  188 us
    all_to_all x1, waiting for transfers between devices, body(): lax.all_to_all(expert_out.reshape(owner_count, -1, model_width), 'ep', sp...  89.2 us
    psum x1, waiting for transfers between devices, body(): lax.psum(arrived.reshape(slot_count, -1).astype(jnp.bfloat16), 'tp')  38.5 us
    all_gather x1, blocking collectives, body(): value_segment = lax.all_gather(value_rows, 'ep', axis=0, tiled=True)  28.8 us
    all_gather x1, blocking collectives, body(): lax.all_gather(merged_local, 'ep', axis=0, tiled=True)  26.2 us
    all_gather x1, blocking collectives, body(): key_segment = lax.all_gather(key_rows, 'ep', axis=0, tiled=True)  22.4 us
    reduce_scatter x1, waiting for transfers between devices, body(): lax.psum_scatter(output.reshape(lax.axis_size('tp') * block_count, flat_i...  18.2 us
    dot_general x1, matrix products, run_experts(): jnp.einsum('nlcf,lfd->nlcd', hidden, down_part, preferred_element_type=jn...  17.2 us
  transfers between devices with their start and end apart: 4, of which 3 were waited for; matrix products, arithmetic and copies ran while one was open for 1% of the time, Pallas kernels for 0%

commit v1 on v0

v1 whole, which is shorter than its diff:
```python
import jax
import jax.numpy as jnp
from jax import lax
from jax.sharding import PartitionSpec as P

HEAD_DIM = 72
MERGE = 4


def attend(query_rows, key_rows, value_rows):
    patch_count = query_rows.shape[0]
    local_heads = query_rows.shape[1] // HEAD_DIM
    score_scale = HEAD_DIM ** (-0.5)
    queries = query_rows.reshape(patch_count, local_heads, HEAD_DIM)
    both = lax.all_gather(jnp.stack([key_rows, value_rows]), "ep", axis=1, tiled=True)
    key_heads = both[0].reshape(-1, local_heads, HEAD_DIM)
    value_heads = both[1].reshape(-1, local_heads, HEAD_DIM)
    scores = (
        jnp.einsum("qhd,khd->hqk", queries, key_heads, preferred_element_type=jnp.float32)
        * score_scale
    )
    weights = jnp.exp(scores - jnp.max(scores, axis=2, keepdims=True))
    sums = jnp.sum(weights, axis=2)
    mixed = jnp.einsum(
        "hqk,khd->hqd", weights.astype(jnp.bfloat16), value_heads, preferred_element_type=jnp.float32
    )
    attended = (mixed / sums[:, :, None]).astype(jnp.bfloat16)
    return attended.transpose(1, 0, 2).reshape(patch_count, local_heads * HEAD_DIM)


def rms(values, norm_gain):
    values = values.astype(jnp.float32)
    scale = lax.rsqrt(jnp.mean(values * values, axis=1, keepdims=True) + 1e-06)
    return (values * scale * norm_gain).astype(jnp.bfloat16)


def body(
    query_rows,
    key_rows,
    value_rows,
    merger_weight,
    visual_counts,
    text_rows,
    norm_gain,
    route_ids,
    route_gates,
    gate_weight,
    up_weight,
    down_weight,
):
    owners = lax.axis_size("ep")
    owner = lax.axis_index("ep")
    patch_count = query_rows.shape[0]
    text_count = text_rows.shape[0]
    row_count = route_ids.shape[0]
    slot_count = row_count - text_count
    local_experts = gate_weight.shape[0]
    expert_count = local_experts * owners
    width = text_rows.shape[1]

    offsets = jnp.cumsum(visual_counts) - visual_counts
    positions = jnp.arange(slot_count, dtype=jnp.int32)
    live = jnp.concatenate(
        [jnp.ones((text_count,), jnp.bool_), positions < visual_counts[owner]]
    )
    named = route_ids[:, :, None] == jnp.arange(expert_count, dtype=jnp.int32)
    grid = jnp.sum(jnp.where(named & live[:, None, None], route_gates[:, :, None], 0.0), axis=1)
    grids = lax.all_to_all(
        grid.reshape(row_count, owners, local_experts).transpose(1, 0, 2),
        "ep", split_axis=0, concat_axis=0, tiled=True,
    )
    sources = offsets[:, None] + positions[None, :]
    filled = positions[None, :] < visual_counts[:, None]
    visual_total = owners * patch_count // MERGE
    pick = (
        filled[:, :, None]
        & (sources[:, :, None] == jnp.arange(visual_total, dtype=jnp.int32))
    )
    text_grid = grids[:, :text_count].reshape(-1, local_experts)
    visual_grid = jnp.einsum(
        "ojv,oje->ve", pick.astype(jnp.float32), grids[:, text_count:],
        precision=lax.Precision.HIGHEST,
    )
    all_grid = jnp.concatenate([text_grid, visual_grid], axis=0)

    text_normed = lax.all_gather(rms(text_rows, norm_gain), "ep", axis=0, tiled=True)

    attended = attend(query_rows, key_rows, value_rows)
    merged = attended.reshape(patch_count // MERGE, -1)
    merged_all = lax.all_gather(merged, "ep", axis=0, tiled=True)
    partial = jnp.dot(
        merged_all, merger_weight.reshape(-1, merger_weight.shape[2]),
        preferred_element_type=jnp.float32,
    )
    half = lax.psum_scatter(partial, "tp", scatter_dimension=0, tiled=True).astype(jnp.bfloat16)
    visual = lax.all_gather(
        lax.all_gather(half, "ep", axis=1, tiled=True), "tp", axis=0, tiled=True
    )
    normed = jnp.concatenate([text_normed, rms(visual, norm_gain)], axis=0)

    total = None
    for e in range(local_experts):
        gate_value = jnp.dot(normed, gate_weight[e], preferred_element_type=jnp.float32)
        up_value = jnp.dot(normed, up_weight[e], preferred_element_type=jnp.float32)
        hidden = jax.nn.silu(gate_value) * up_value * all_grid[:, e : e + 1]
        term = jnp.dot(
            hidden.astype(jnp.bfloat16), down_weight[e], preferred_element_type=jnp.float32
        )
        total = term if total is None else total + term
    total = total.astype(jnp.bfloat16)
    slot_sum = jnp.einsum(
        "ojv,vd->ojd", pick.astype(jnp.bfloat16), total[owners * text_count :],
        preferred_element_type=jnp.float32,
    ).astype(jnp.bfloat16)
    owned = jnp.concatenate(
        [total[: owners * text_count].reshape(owners, text_count, width), slot_sum], axis=1
    ).reshape(-1, width)
    combined = lax.psum_scatter(owned, ("ep", "tp"), scatter_dimension=0, tiled=True)
    my_visual = jnp.dot(
        pick[owner].astype(jnp.bfloat16), visual, preferred_element_type=jnp.float32
    ).astype(jnp.bfloat16)
    rows = jnp.concatenate([text_rows, my_visual], axis=0)
    share = row_count // lax.axis_size("tp")
    residual = lax.dynamic_slice_in_dim(rows, lax.axis_index("tp") * share, share, 0)
    out = (residual.astype(jnp.float32) + combined.astype(jnp.float32)).astype(jnp.bfloat16)
    return lax.all_gather(out, "tp", axis=0, tiled=True)


def solution(mesh):
    return jax.shard_map(
        body,
        mesh=mesh,
        in_specs=(
            P(("grp", "ep"), "tp"),
            P(("grp", "ep"), "tp"),
            P(("grp", "ep"), "tp"),
            P(None, "tp", "ep"),
            P("grp"),
            P(("grp", "ep"), None),
            P(),
            P(("grp", "ep"), None),
            P(("grp", "ep"), None),
            P("ep", None, "tp"),
            P("ep", None, "tp"),
            P("ep", "tp", None),
        ),
        out_specs=P(("grp", "ep"), None),
        check_vma=False,
    )
```

time: 534 us -> 341 us (0.64)
  blocking collectives: 268 us -> 49.7 us
  waiting for transfers between devices: 146 us -> 181 us
  matrix products: 35.7 us -> 61.8 us
  local copies, waits for them, and re-layouts: 33.3 us -> 11 us
  other arithmetic: 18.8 us -> 12.7 us
    all_to_all x1 -> x0, blocking collectives: 188 us -> none  [body(): lax.all_to_all(packed, 'ep', split_axis=1, concat_axis=1, tiled=True)]
    all_gather x0 -> x3, waiting for transfers between devices: none -> 92.4 us  [the longest x1 47.8 us: body(): lax.all_gather(rms(text_rows, norm_gain), 'ep', axis=0, tiled=True)]
    all_to_all x2 -> x1, waiting for transfers between devices: 89.2 us -> 2.94 us  [body(): lax.all_to_all(grid.reshape(row_count, owners, local_experts).transpose(1...]
    reduce_scatter x1 -> x2, waiting for transfers between devices: 18.2 us -> 85.3 us  [the longest x1 67.3 us: body(): lax.psum_scatter(owned, ('ep', 'tp'), scatter_dimension=0, tiled=True)]
    psum x1 -> x0, waiting for transfers between devices: 38.5 us -> none  [body(): lax.psum(arrived.reshape(slot_count, -1).astype(jnp.bfloat16), 'tp')]
    all_gather x4 -> x3, blocking collectives: 80.6 us -> 49.7 us  [the longest x1 23.2 us: body(): lax.all_gather(half, 'ep', axis=1, tiled=True)]
    dot_general x7 -> x14, matrix products: 35.7 us -> 61.8 us  [the longest x4 40.5 us: body(): jnp.dot(hidden.astype(jnp.bfloat16), down_weight[e], preferred_element_ty...]
    gather x2 -> x0, local copies, waits for them, and re-layouts: 9.24 us -> none  [the longest x1 8.09 us: body(): picked = returned[jnp.maximum(own_slots, 0)]]
  transfers between devices with their start and end apart: 4 -> 6, of which waited for: 3 -> 6; matrix products, arithmetic and copies ran while one was open for 1% -> 3% of each run, Pallas kernels for 0% -> 0%
where the time goes in v1:
time: 341 us; the launch traced here: 339 us
  waiting for transfers between devices  181 us (53%)
  matrix products  61.8 us (18%)
  blocking collectives  49.7 us (15%)
  between operations  13.4 us (4%)
  other arithmetic  12.7 us (4%)
  local copies, waits for them, and re-layouts  11 us (3%)
  starting transfers between devices  9.36 us (3%)
    reduce_scatter x1, waiting for transfers between devices, body(): lax.psum_scatter(owned, ('ep', 'tp'), scatter_dimension=0, tiled=True)  67.3 us
    all_gather x1, waiting for transfers between devices, body(): lax.all_gather(rms(text_rows, norm_gain), 'ep', axis=0, tiled=True)  47.8 us
    all_gather x1, waiting for transfers between devices, attend(): lax.all_gather(jnp.stack([key_rows, value_rows]), 'ep', axis=1, tiled=True)  41.4 us
    dot_general x4, matrix products, body(): jnp.dot(hidden.astype(jnp.bfloat16), down_weight[e], preferred_element_ty...  40.5 us
    all_gather x1, blocking collectives, body(): lax.all_gather(half, 'ep', axis=1, tiled=True)  23.2 us
    all_gather x1, blocking collectives, body(): merged_all = lax.all_gather(merged, 'ep', axis=0, tiled=True)  22.4 us
    reduce_scatter x1, waiting for transfers between devices, body(): lax.psum_scatter(partial, 'tp', scatter_dimension=0, tiled=True)  18 us
    dot_general x4, matrix products, body(): jnp.dot(normed, gate_weight[e], preferred_element_type=jnp.float32)  15.2 us
  transfers between devices with their start and end apart: 6, of which 6 were waited for; matrix products, arithmetic and copies ran while one was open for 3% of the time, Pallas kernels for 0%

profile of v1, /device:TPU:17, one launch (start us, length us, event | category | flops | bytes accessed | tf_op | source)
XLA Modules:
  0.0 338.6 jit_solution(1485964103713605444)
XLA Ops:
  6.5 1.8 pad_maximum_fusion.2
  8.3 0.0 all-gather.4.cloned.1.call-update
  8.3 0.0 reduce-scatter.3.cloned.1.call-start
  8.4 1.0 reshape.110
  9.4 41.4 %all-gather.4.cloned.1.call-done = bf16[2,512,576]{2,1,0:T(8,128)(2,1)} async-done(((bf16[2,64,576]{2,1,0:T(8,128)(2,1)}), bf16[2,512,576]{2,1,0:T(8,128)(2,1)}) %all-gather.4.cloned.1.call-update) | async-done | bytes 1179664 | tf_op jit(solution)/shard_map/all_gather | solution.py:15
  50.8 2.3 fusion.139
  53.1 2.1 copy.26
  55.2 1.1 copy.28
  56.3 1.4 fusion.140
  57.7 0.4 fusion.83
  58.1 1.5 fusion.82
  59.5 0.0 copy-start.6
  59.5 0.1 copy.29
  59.6 0.2 reshape_reshape.3
  59.9 0.0 copy-start.7
  59.9 22.4 %all_gather.19 = bf16[128,2304]{1,0:T(8,128)(2,1)S(1)} all-gather(bf16[16,2304]{1,0:T(8,128)(2,1)S(1)} %reshape_reshape.3), channel_id=1, replica_groups=mesh['grp'=2,'ep'=8,'tp'=2] {'ep'}, dimensions={0}, use_global_device_ids=true | all-gather | bytes 663552 | tf_op jit(solution)/shard_map/all_gather | solution.py:90
  82.3 1.2 fusion.141
  83.5 0.0 reduce-scatter.3.cloned.1.call-update
  83.5 0.0 all-gather.6.cloned.1.call-start
  83.6 0.2 fusion.105
  83.7 18.0 %reduce-scatter.3.cloned.1.call-done = f32[64,512]{1,0:T(8,128)} async-done(((f32[128,512]{1,0:T(8,128)}), f32[64,512]{1,0:T(8,128)}) %reduce-scatter.3.cloned.1.call-update) | async-done | bytes 131088 | tf_op jit(solution)/shard_map/reduce_scatter | solution.py:95
  101.7 0.9 convert_element_type.57
  102.7 23.2 %all_gather.20 = bf16[64,4096]{1,0:T(8,128)(2,1)} all-gather(bf16[64,512]{1,0:T(8,128)(2,1)S(1)} %convert_element_type.57), channel_id=1, replica_groups=mesh['grp'=2,'ep'=8,'tp'=2] {'ep'}, dimensions={1}, use_global_device_ids=true | all-gather | bytes 589824 | tf_op jit(solution)/shard_map/all_gather | solution.py:97
  125.8 0.0 all-gather.6.cloned.1.call-update
  125.9 0.0 all-gather.8.cloned.1.call-start
  125.9 0.8 fusion.107
  126.8 0.0 all-gather.8.cloned.1.call-update
  126.8 0.7 dynamic_slice.11
  127.5 0.7 iota_compare_fusion.3
  128.2 0.1 concatenate.17
  128.3 0.7 reshape.122
  129.0 9.2 %all-to-all-start = ((f32[8,1,256]{2,1,0:T(1,128)}), f32[8,1,256]{2,1,0:T(1,128)S(1)}, u32[]{:S(2)}, u32[]{:S(2)}) async-start(f32[8,1,256]{2,1,0:T(1,128)} %reshape.122), calls=%async_computation.1 | async-start | bytes 16384 | tf_op jit(solution)/shard_map/all_to_all | solution.py:68
  138.2 0.2 reduce-window.9
  138.4 0.1 iota_add_fusion
  138.5 0.1 iota_compare_fusion.2
  138.6 2.9 all-to-all-done
  141.5 0.6 broadcast.69
  142.1 0.7 reduce.8
  142.8 0.1 reshape.123
  142.9 0.1 reshape.113
  143.0 0.3 convolution_bitcast_fusion.1
  143.3 3.2 all-gather.6.cloned.1.call-done
  146.5 1.5 fusion.35
  148.0 1.6 fusion.37
  149.6 47.8 %all-gather.8.cloned.1.call-done = bf16[256,4096]{1,0:T(8,128)(2,1)} async-done(((bf16[32,4096]{1,0:T(8,128)(2,1)}), bf16[256,4096]{1,0:T(8,128)(2,1)}) %all-gather.8.cloned.1.call-update) | async-done | bytes 2097168 | tf_op jit(solution)/shard_map/all_gather | solution.py:86
  197.4 5.3 %fusion.15 = f32[384,384]{1,0:T(8,128)} fusion(bf16[4,4096,384]{2,1,0:T(8,128)(2,1)} %param.21, bf16[128,4096]{1,0:T(8,128)(2,1)S(1)} %fusion.37, bf16[256,4096]{1,0:T(8,128)(2,1)} %all-gather.8.cloned.1.call-done), kind=kOutput, calls=%fused_computation.20 | convolution fusion | flops 1214251008 | bytes 6881280 | tf_op jit(solution)/shard_map/dot_general | solution.py:103
  202.6 4.7 %fusion.9 = f32[384,384]{1,0:T(8,128)} fusion(bf16[4,4096,384]{2,1,0:T(8,128)(2,1)} %param.21, bf16[128,4096]{1,0:T(8,128)(2,1)S(1)} %fusion.37, bf16[256,4096]{1,0:T(8,128)(2,1)S(1)} %copy-done.5), kind=kOutput, calls=%fused_computation.14 | convolution fusion | flops 1214251008 | bytes 6881280 | tf_op jit(solution)/shard_map/dot_general | solution.py:103
  207.3 2.6 fusion.3
  210.0 2.7 fusion.21
  212.6 9.2 %fusion.17 = f32[384,4096]{1,0:T(8,128)} fusion(bf16[4,384,4096]{2,1,0:T(8,128)(2,1)} %param.23, bf16[4,4096,384]{2,1,0:T(8,128)(2,1)} %param.22, f32[384,384]{1,0:T(8,128)} %fusion.21, f32[384]{0:T(512)S(1)} %get-tuple-element.6, bf16[128,4096]{1,0:T(8,128)(2,1)S(1)} %fusion.37, bf16[256,4096]{1,0:T(8,128)(2,1)S(1)} %copy-done.5), kind=kOutput, calls=%fused_computation.22 | convolution fusion | flops 2423242752 | bytes 16320000 | tf_op jit(solution)/shard_map/dot_general | solution.py:106
  221.8 9.2 %fusion.5 = f32[384,4096]{1,0:T(8,128)} fusion(bf16[4,384,4096]{2,1,0:T(8,128)(2,1)} %param.23, bf16[4,4096,384]{2,1,0:T(8,128)(2,1)} %param.22, f32[384,384]{1,0:T(8,128)} %fusion.9, f32[384]{0:T(512)S(1)} %get-tuple-element.8, bf16[128,4096]{1,0:T(8,128)(2,1)S(1)} %fusion.37, bf16[256,4096]{1,0:T(8,128)(2,1)S(1)} %copy-done.5), kind=kOutput, calls=%fused_computation.10 | convolution fusion | flops 2423242752 | bytes 16320000 | tf_op jit(solution)/shard_map/dot_general | solution.py:106
  231.0 9.4 %fusion.11 = f32[384,4096]{1,0:T(8,128)} fusion(bf16[4,384,4096]{2,1,0:T(8,128)(2,1)} %param.23, bf16[4,4096,384]{2,1,0:T(8,128)(2,1)} %param.22, f32[384,384]{1,0:T(8,128)} %fusion.15, f32[384]{0:T(512)S(1)} %get-tuple-element.7, bf16[128,4096]{1,0:T(8,128)(2,1)S(1)} %fusion.37, bf16[256,4096]{1,0:T(8,128)(2,1)S(1)} %copy-done.5), kind=kOutput, calls=%fused_computation.16 | convolution fusion | flops 2423242752 | bytes 16320000 | tf_op jit(solution)/shard_map/dot_general | solution.py:106
  240.4 12.8 %add_convert_fusion = bf16[384,4096]{1,0:T(8,128)(2,1)S(1)} fusion(f32[384,4096]{1,0:T(8,128)} %fusion.5, f32[384,4096]{1,0:T(8,128)} %fusion.17, f32[384,4096]{1,0:T(8,128)} %fusion.11, bf16[4,384,4096]{2,1,0:T(8,128)(2,1)} %param.23, bf16[4,4096,384]{2,1,0:T(8,128)(2,1)} %param.22, f32[384,384]{1,0:T(8,128)} %fusion.3, f32[384]{0:T(512)S(1)} %get-tuple-element.5, ...), kind=kOutput, calls=%fused_computation | convolution fusion | flops 2429534208 | bytes 32048640 | tf_op jit(solution)/shard_map/dot_general | solution.py:106
  253.2 0.8 convolution_convert_fusion
  253.9 0.1 slice.98
  254.1 2.4 pad_maximum_fusion
  256.5 0.0 reduce-scatter.5.cloned.1.call-update
  256.5 0.1 fusion.120
  256.7 1.0 copy-done.2
  257.7 1.0 convolution_convert_fusion.1
  258.7 67.3 %reduce-scatter.5.cloned.1.call-done = bf16[32,4096]{1,0:T(8,128)(2,1)} async-done(((bf16[512,4096]{1,0:T(8,128)(2,1)}), bf16[32,4096]{1,0:T(8,128)(2,1)}) %reduce-scatter.5.cloned.1.call-update) | async-done | bytes 262160 | tf_op jit(solution)/shard_map/reduce_scatter | solution.py:118
  326.0 1.2 add_convert_fusion.1
  327.2 4.1 %all_gather.23 = bf16[64,4096]{1,0:T(8,128)(2,1)S(1)} all-gather(bf16[32,4096]{1,0:T(8,128)(2,1)S(1)} %add_convert_fusion.1), channel_id=1, replica_groups=mesh['grp'=2,'ep'=8,'tp'=2] {'tp'}, dimensions={0}, use_global_device_ids=true | all-gather | bytes 786432 | tf_op jit(solution)/shard_map/all_gather | solution.py:126
  331.3 0.8 copy.38
  (32 shorter events, 0.2 us)
Async XLA Ops:
  6.5 75.8 %copy-start = (bf16[4,576,512]{2,1,0:T(8,128)(2,1)S(1)}, bf16[4,576,512]{2,1,0:T(8,128)(2,1)}, u32[]{:S(2)}) copy-start(bf16[4,576,512]{2,1,0:T(8,128)(2,1)} %param.15) | copy-start | bytes 7077892
  6.5 44.3 %all-gather.4.cloned.1.call-start = ((), (), s32[]{:S(2)}) async-start(), calls=%async_computation.3 | async-start | bytes 1474560 | tf_op jit(solution)/shard_map/all_gather | solution.py:15
  8.3 93.4 %reduce-scatter.3.cloned.1.call-start = ((), (), s32[]{:S(2)}) async-start(), calls=%async_computation.4 | async-start | bytes 393216 | tf_op jit(solution)/shard_map/reduce_scatter | solution.py:95
  58.0 25.5 %copy-start.4 = (bf16[32,4096]{1,0:T(8,128)(2,1)S(1)}, bf16[32,4096]{1,0:T(8,128)(2,1)}, u32[]{:S(2)}) copy-start(bf16[32,4096]{1,0:T(8,128)(2,1)} %param.17) | copy-start | bytes 786436
  59.5 66.4 %copy-start.6 = (f32[4096]{0:T(1024)S(1)}, f32[4096]{0:T(1024)}, u32[]{:S(2)}) copy-start(f32[4096]{0:T(1024)} %param.18) | copy-start | bytes 49156
  59.8 67.0 %copy-start.9 = (s32[8]{0:T(128)S(1)}, s32[8]{0:T(128)}, u32[]{:S(2)}) copy-start(s32[8]{0:T(128)} %param.16) | copy-start | bytes 100
  59.9 68.4 %copy-start.7 = (f32[64,8]{0,1:T(8,128)S(1)}, f32[64,8]{0,1:T(8,128)}, u32[]{:S(2)}) copy-start(f32[64,8]{0,1:T(8,128)} %param.20) | copy-start | bytes 6148
  59.9 68.4 %copy-start.8 = (s32[64,8]{0,1:T(8,128)S(1)}, s32[64,8]{0,1:T(8,128)}, u32[]{:S(2)}) copy-start(s32[64,8]{0,1:T(8,128)} %param.19) | copy-start | bytes 6148
  83.5 63.0 %all-gather.6.cloned.1.call-start = ((), (), s32[]{:S(2)}) async-start(), calls=%async_computation.5 | async-start | bytes 1572864 | tf_op jit(solution)/shard_map/all_gather | solution.py:96
  125.9 71.5 %all-gather.8.cloned.1.call-start = ((), (), s32[]{:S(2)}) async-start(), calls=%async_computation.6 | async-start | bytes 2359296 | tf_op jit(solution)/shard_map/all_gather | solution.py:86
  129.0 12.5 %all-to-all-start = ((f32[8,1,256]{2,1,0:T(1,128)}), f32[8,1,256]{2,1,0:T(1,128)S(1)}, u32[]{:S(2)}, u32[]{:S(2)}) async-start(f32[8,1,256]{2,1,0:T(1,128)} %reshape.122), calls=%async_computation.1 | async-start | bytes 16384 | tf_op jit(solution)/shard_map/all_to_all | solution.py:68
  138.2 187.8 %reduce-scatter.5.cloned.1.call-start = ((), (), s32[]{:S(2)}) async-start(), calls=%async_computation.7 | async-start | bytes 4456448 | tf_op jit(solution)/shard_map/reduce_scatter | solution.py:118
  149.6 81.4 %copy-start.3 = (bf16[128,4096]{1,0:T(8,128)(2,1)}, bf16[128,4096]{1,0:T(8,128)(2,1)S(1)}, u32[]{:S(2)}) copy-start(bf16[128,4096]{1,0:T(8,128)(2,1)S(1)} %fusion.37) | copy-start | bytes 3145732
  197.4 5.3 %copy-start.5 = (bf16[256,4096]{1,0:T(8,128)(2,1)S(1)}, bf16[256,4096]{1,0:T(8,128)(2,1)}, u32[]{:S(2)}) copy-start(bf16[256,4096]{1,0:T(8,128)(2,1)} %all-gather.8.cloned.1.call-done) | copy-start | bytes 6291460
  197.4 9.9 %slice-start = ((s8[12582912]{0:T(1024)(128)(4,1)}), s8[4194304]{0:T(1024)(128)(4,1)S(1)}, s32[]{:S(2)}) async-start(s8[12582912]{0:T(1024)(128)(4,1)} %bitcast.120), calls=%async_computation.8 | async-start | bytes 8388608
  197.4 9.9 %slice-start.1 = ((s8[12582912]{0:T(1024)(128)(4,1)}), s8[4194304]{0:T(1024)(128)(4,1)S(1)}, s32[]{:S(2)}) async-start(s8[12582912]{0:T(1024)(128)(4,1)} %bitcast.120), calls=%async_computation.9 | async-start | bytes 8388608
  202.6 4.7 %slice-start.2 = ((s8[12582912]{0:T(1024)(128)(4,1)}), s8[4194304]{0:T(1024)(128)(4,1)S(1)}, s32[]{:S(2)}) async-start(s8[12582912]{0:T(1024)(128)(4,1)} %bitcast.120), calls=%async_computation.10 | async-start | bytes 8388608
  256.5 1.2 copy-start.2
  256.5 75.5 %copy-start.1 = (bf16[4,576,512]{2,1,0:T(8,128)(2,1)S(1)}, bf16[4,576,512]{2,1,0:T(8,128)(2,1)}, u32[]{:S(2)}) copy-start(bf16[4,576,512]{2,1,0:T(8,128)(2,1)} %param.15) | copy-start | bytes 7077892
Sparse Core Ops, SparseCore 0:
  9.6 41.2 all-gather.3
  83.6 18.0 reduce-scatter.2
  126.0 20.4 all-gather.5
  148.7 48.6 all-gather.7
  256.7 69.3 reduce-scatter.4

commit v2 on v1

--- a/solution.py
+++ b/solution.py
@@ -1,37 +1,299 @@
+import functools
+
 import jax
 import jax.numpy as jnp
 from jax import lax
+from jax.experimental import pallas as pl
+from jax.experimental.pallas import tpu as pltpu
 from jax.sharding import PartitionSpec as P
 
 HEAD_DIM = 72
 MERGE = 4
-
-
-def attend(query_rows, key_rows, value_rows):
-    patch_count = query_rows.shape[0]
-    local_heads = query_rows.shape[1] // HEAD_DIM
-    score_scale = HEAD_DIM ** (-0.5)
-    queries = query_rows.reshape(patch_count, local_heads, HEAD_DIM)
-    both = lax.all_gather(jnp.stack([key_rows, value_rows]), "ep", axis=1, tiled=True)
-    key_heads = both[0].reshape(-1, local_heads, HEAD_DIM)
-    value_heads = both[1].reshape(-1, local_heads, HEAD_DIM)
-    scores = (
-        jnp.einsum("qhd,khd->hqk", queries, key_heads, preferred_element_type=jnp.float32)
-        * score_scale
-    )
-    weights = jnp.exp(scores - jnp.max(scores, axis=2, keepdims=True))
-    sums = jnp.sum(weights, axis=2)
-    mixed = jnp.einsum(
-        "hqk,khd->hqd", weights.astype(jnp.bfloat16), value_heads, preferred_element_type=jnp.float32
-    )
-    attended = (mixed / sums[:, :, None]).astype(jnp.bfloat16)
-    return attended.transpose(1, 0, 2).reshape(patch_count, local_heads * HEAD_DIM)
+MESH = pl.DeviceIdType.MESH
+MIB = 1 << 20
+
+
+class TreeGather:
+    def __init__(self, block, count, send_sem, recv_sem):
+        self.block, self.send_sem, self.recv_sem = block, send_sem, recv_sem
+        me = lax.axis_index("ep")
+        self.a, self.b, self.line = me // 2, me % 2, count // 2
+
+    def copy(self, half, a, b, way):
+        target = (
+            (self.a + 1) * 2 + self.b,
+            (self.a - 1) * 2 + self.b,
+            self.a * 2 + 1 - self.b,
+        )[way]
+        target = jnp.clip(target, 0, 2 * self.line - 1)
+        slot = a * 2 + b
+        return pltpu.make_async_remote_copy(
+            src_ref=self.block(half, slot),
+            dst_ref=self.block(half, slot),
+            send_sem=self.send_sem.at[half, slot, way],
+            recv_sem=self.recv_sem.at[half, slot],
+            device_id={"ep": target},
+            device_id_type=MESH,
+        )
+
+    def recv(self, half, a, b):
+        self.copy(half, a, b, 2).wait_recv()
+
+    def right(self, half, a, b, act):
+        @pl.when(self.a < self.line - 1)
+        def _():
+            act(self.copy(half, a, b, 0))
+
+    def left(self, half, a, b, act):
+        @pl.when(self.a > 0)
+        def _():
+            act(self.copy(half, a, b, 1))
+
+    def start(self, act=lambda c: c.start()):
+        act(self.copy(0, self.a, self.b, 2))
+        act(self.copy(1, self.a, self.b, 2))
+        for half in range(2):
+            self.right(half, self.a, self.b, act)
+            self.left(half, self.a, self.b, act)
+
+    def cross(self):
+        self.recv(1, self.a, 1 - self.b)
+        for go in (self.right, self.left):
+            go(1, self.a, 1 - self.b, lambda c: c.start())
+
+    def step(self, d, act=lambda c: c.start(), receive=True):
+        for half, column in ((0, self.b), (1, self.b), (1, 1 - self.b)):
+
+            @pl.when(self.a >= d)
+            def _():
+                if receive:
+                    self.recv(half, self.a - d, column)
+                self.right(half, self.a - d, column, act)
+                if half == 0:
+                    act(self.copy(half, self.a - d, column, 2))
+
+            @pl.when(self.a + d < self.line)
+            def _():
+                if receive:
+                    self.recv(half, self.a + d, column)
+                self.left(half, self.a + d, column, act)
+                if half == 0:
+                    act(self.copy(half, self.a + d, column, 2))
+
+    def finish(self):
+        for other in range(self.line):
+            self.recv(0, other, 1 - self.b)
+        wait = lambda c: c.wait_send()
+        self.start(wait)
+        for go in (self.right, self.left):
+            go(1, self.a, 1 - self.b, wait)
+        for d in range(1, self.line):
+            self.step(d, wait, False)
+
+
+def greet(count):
+    barrier = pltpu.get_barrier_semaphore()
+    me, core = lax.axis_index("ep"), lax.axis_index("tp")
+    line = count // 2
+    a, b = me // 2, me % 2
+
+    def say(ids):
+        pl.semaphore_signal(barrier, inc=1, device_id=ids, device_id_type=MESH)
+
+    say({"tp": 1 - core})
+    say({"ep": a * 2 + 1 - b})
+
+    @pl.when(a < line - 1)
+    def _():
+        say({"ep": jnp.minimum(a + 1, line - 1) * 2 + b})
+
+    @pl.when(a > 0)
+    def _():
+        say({"ep": jnp.maximum(a - 1, 0) * 2 + b})
+
+    edges = jnp.where(a < line - 1, 1, 0) + jnp.where(a > 0, 1, 0)
+    pl.semaphore_wait(barrier, 2 + edges)
+
+
+def to_partner(src, dst, send_sem, recv_sem):
+    return pltpu.make_async_remote_copy(
+        src_ref=src,
+        dst_ref=dst,
+        send_sem=send_sem,
+        recv_sem=recv_sem,
+        device_id={"tp": 1 - lax.axis_index("tp")},
+        device_id_type=MESH,
+    )
 
 
 def rms(values, norm_gain):
     values = values.astype(jnp.float32)
     scale = lax.rsqrt(jnp.mean(values * values, axis=1, keepdims=True) + 1e-06)
     return (values * scale * norm_gain).astype(jnp.bfloat16)
+
+
+def front_kernel(
+    count,
+    query, key, value, weight, text_ref, gain, grid_ref,
+    normed_out, visual_out, grid_out,
+    kv, text, att, vis, grid, part, part_in,
+    kv_send, kv_recv, text_send, text_recv, att_send, att_recv, vis_send, vis_recv,
+    grid_send, grid_recv, pair_send, pair_recv,
+):
+    me, core = lax.axis_index("ep"), lax.axis_index("tp")
+    line = count // 2
+    kv_gather = TreeGather(lambda h, s: kv.at[h, s], count, kv_send, kv_recv)
+    text_gather = TreeGather(lambda h, s: text.at[core, h, s], count, text_send, text_recv)
+    att_gather = TreeGather(lambda h, s: att.at[h, s], count, att_send, att_recv)
+    vis_gather = TreeGather(lambda h, s: vis.at[core, h, s], count, vis_send, vis_recv)
+    grid_gather = TreeGather(lambda h, s: grid.at[h, s], count, grid_send, grid_recv)
+
+    kv[0, me] = key[...]
+    kv[1, me] = value[...]
+    greet(count)
+    kv_gather.start()
+    width = text_ref.shape[1]
+    mine = text_ref.shape[0] // 2
+    own = rms(text_ref[pl.ds(pl.multiple_of(core * mine, mine), mine), :], gain[...])
+    text[core, 0, me] = own[:, : width // 2]
+    text[core, 1, me] = own[:, width // 2 :]
+    grid[0, me] = grid_ref[0]
+    grid[1, me] = grid_ref[1]
+    kv_gather.cross()
+    for d in range(1, line):
+        kv_gather.step(d)
+        if d == 1:
+            grid_gather.start()
+            text_gather.start()
+    kv_gather.finish()
+    grid_gather.cross()
+    text_gather.cross()
+    text_gather.step(1)
+    grid_gather.step(1)
+
+    patches, features = query.shape
+    keys = kv[0].reshape(count * patches, features)
+    values = kv[1].reshape(count * patches, features)
+    parts = []
+    for head in range(features // HEAD_DIM):
+        lanes = slice(head * HEAD_DIM, (head + 1) * HEAD_DIM)
+        scores = lax.dot_general(
+            query[:, lanes], keys[:, lanes], (((1,), (1,)), ((), ())),
+            preferred_element_type=jnp.float32,
+        ) * (HEAD_DIM ** (-0.5))
+        weights = jnp.exp(scores - jnp.max(scores, axis=1, keepdims=True))
+        sums = jnp.sum(weights, axis=1, keepdims=True)
+        mixed = jnp.dot(
+            weights.astype(jnp.bfloat16), values[:, lanes], preferred_element_type=jnp.float32
+        )
+        parts.append((mixed / sums).astype(jnp.bfloat16))
+    attended = jnp.concatenate(parts, axis=1)
+    rows = patches // MERGE
+    for p in range(MERGE):
+        att[p // 2, me, p % 2] = attended[p * rows : (p + 1) * rows]
+    att_gather.start()
+    late = [d for d in range(2, line)]
+    for d in late[: len(late) // 2]:
+        text_gather.step(d)
+    att_gather.cross()
+    for d in range(1, line):
+        att_gather.step(d)
+    for d in late[len(late) // 2 :]:
+        text_gather.step(d)
+    for d in late:
+        grid_gather.step(d)
+    att_gather.finish()
+
+    total = None
+    for p in range(MERGE):
+        left = att[p // 2, :, p % 2].reshape(count * rows, features)
+        term = jnp.dot(left, weight[p], preferred_element_type=jnp.float32)
+        total = term if total is None else total + term
+    half_rows = count * rows // 2
+    part[0] = total[:half_rows]
+    part[1] = total[half_rows:]
+    swap = to_partner(part.at[1 - core], part_in, pair_send.at[0], pair_recv.at[0])
+    swap.start()
+    swap.wait()
+    summed = (part[core] + part_in[...]).astype(jnp.bfloat16)
+    quarter = half_rows // 2
+    vis[core, 0, me] = summed[:quarter]
+    vis[core, 1, me] = summed[quarter:]
+    vis_gather.start()
+    text_gather.finish()
+    swap_text = to_partner(text.at[core], text.at[core], pair_send.at[1], pair_recv.at[1])
+    swap_text.start()
+    vis_gather.cross()
+    for d in range(1, line):
+        vis_gather.step(d)
+    grid_gather.finish()
+    for s in range(count):
+        for h in range(2):
+            grid_out[s, h] = grid[h, s]
+    vis_gather.finish()
+    swap_vis = to_partner(vis.at[core], vis.at[core], pair_send.at[2], pair_recv.at[2])
+    swap_vis.start()
+    swap_text.wait_send()
+    to_partner(text.at[1 - core], text.at[1 - core], pair_send.at[1], pair_recv.at[1]).wait_recv()
+    for s in range(count):
+        for c in range(2):
+            for h in range(2):
+                normed_out[
+                    s * 2 * mine + c * mine : s * 2 * mine + (c + 1) * mine,
+                    h * width // 2 : (h + 1) * width // 2,
+                ] = text[c, h, s]
+    swap_vis.wait_send()
+    to_partner(vis.at[1 - core], vis.at[1 - core], pair_send.at[2], pair_recv.at[2]).wait_recv()
+    columns = weight.shape[2]
+    base = count * 2 * mine
+    for c in range(2):
+        for h in range(2):
+            first = (c * 2 + h) * quarter
+            for s in range(count):
+                visual_out[first : first + quarter, s * columns : (s + 1) * columns] = vis[c, h, s]
+            normed_out[base + first : base + first + quarter, :] = rms(
+                visual_out[first : first + quarter, :], gain[...]
+            )
+
+
+def front(query_rows, key_rows, value_rows, merger_weight, text_rows, norm_gain, grid):
+    count = lax.axis_size("ep")
+    patches, features = query_rows.shape
+    rows = patches // MERGE
+    text_count, width = text_rows.shape
+    columns = merger_weight.shape[2]
+    quarter = count * rows // 4
+    queries = query_rows.reshape(rows, MERGE, features).transpose(1, 0, 2).reshape(patches, features)
+    bf16, f32 = jnp.bfloat16, jnp.float32
+    sems = []
+    for _ in range(5):
+        sems += [pltpu.SemaphoreType.DMA((2, count, 3)), pltpu.SemaphoreType.DMA((2, count))]
+    vmem = pl.BlockSpec(memory_space=pltpu.VMEM)
+    return pl.pallas_call(
+        functools.partial(front_kernel, count),
+        name="front",
+        out_shape=(
+            jax.ShapeDtypeStruct((count * (text_count + rows), width), bf16),
+            jax.ShapeDtypeStruct((count * rows, width), bf16),
+            jax.ShapeDtypeStruct((count,) + grid.shape, f32),
+        ),
+        in_specs=[vmem] * 7,
+        out_specs=(vmem,) * 3,
+        scratch_shapes=[
+            pltpu.VMEM((2, count, patches, features), bf16),
+            pltpu.VMEM((2, 2, count, text_count // 2, width // 2), bf16),
+            pltpu.VMEM((2, count, 2, rows, features), bf16),
+            pltpu.VMEM((2, 2, count, quarter, columns), bf16),
+            pltpu.VMEM((2, count) + grid.shape[1:], f32),
+            pltpu.VMEM((2, 2 * quarter, columns), f32),
+            pltpu.VMEM((2 * quarter, columns), f32),
+        ]
+        + sems
+        + [pltpu.SemaphoreType.DMA((3,)), pltpu.SemaphoreType.DMA((3,))],
+        compiler_params=pltpu.CompilerParams(
+            collective_id=0, has_side_effects=True, vmem_limit_bytes=56 * MIB
+        ),
+    )(queries, key_rows, value_rows, merger_weight, text_rows, norm_gain.reshape(1, -1), grid)
 
 
 def body(
@@ -65,10 +327,14 @@
     )
     named = route_ids[:, :, None] == jnp.arange(expert_count, dtype=jnp.int32)
     grid = jnp.sum(jnp.where(named & live[:, None, None], route_gates[:, :, None], 0.0), axis=1)
-    grids = lax.all_to_all(
-        grid.reshape(row_count, owners, local_experts).transpose(1, 0, 2),
-        "ep", split_axis=0, concat_axis=0, tiled=True,
-    )
+    flat = jnp.pad(grid.T, ((0, 0), (0, -row_count % 128)))
+    flat = flat.reshape(2, expert_count // 2, -1)
+    normed, visual, grids = front(
+        query_rows, key_rows, value_rows, merger_weight, text_rows, norm_gain, flat
+    )
+    grids = grids.reshape(owners, owners, local_experts, -1)
+    grids = lax.dynamic_index_in_dim(grids, owner, 1, False)[:, :, :row_count]
+    grids = grids.transpose(0, 2, 1)
     sources = offsets[:, None] + positions[None, :]
     filled = positions[None, :] < visual_counts[:, None]
     visual_total = owners * patch_count // MERGE
@@ -82,21 +348,6 @@
         precision=lax.Precision.HIGHEST,
     )
     all_grid = jnp.concatenate([text_grid, visual_grid], axis=0)
-
-    text_normed = lax.all_gather(rms(text_rows, norm_gain), "ep", axis=0, tiled=True)
-
-    attended = attend(query_rows, key_rows, value_rows)
-    merged = attended.reshape(patch_count // MERGE, -1)
-    merged_all = lax.all_gather(merged, "ep", axis=0, tiled=True)
-    partial = jnp.dot(
-        merged_all, merger_weight.reshape(-1, merger_weight.shape[2]),
-        preferred_element_type=jnp.float32,
-    )
-    half = lax.psum_scatter(partial, "tp", scatter_dimension=0, tiled=True).astype(jnp.bfloat16)
-    visual = lax.all_gather(
-        lax.all_gather(half, "ep", axis=1, tiled=True), "tp", axis=0, tiled=True
-    )
-    normed = jnp.concatenate([text_normed, rms(visual, norm_gain)], axis=0)
 
     total = None
     for e in range(local_experts):

time: 341 us -> 225 us (0.66)
  waiting for transfers between devices: 181 us -> 68.9 us
  Pallas kernels: 0 us -> 66.2 us
  blocking collectives: 49.7 us -> 4.1 us
  starting transfers between devices: 9.36 us -> 0.01 us
  other arithmetic: 12.7 us -> 6.06 us
  local copies, waits for them, and re-layouts: 11 us -> 6.29 us
  matrix products: 61.8 us -> 57.7 us
    all_gather x3 -> x0, waiting for transfers between devices: 92.4 us -> none  [the longest x1 47.8 us: body(): lax.all_gather(rms(text_rows, norm_gain), 'ep', axis=0, tiled=True)]
    pallas_call x0 -> x1, Pallas kernels: none -> 66.2 us  [front(): pl.pallas_call(functools.partial(front_kernel, count), name='front', out_...]
    all_gather x2 -> x0, blocking collectives: 45.6 us -> none  [the longest x1 23.2 us: body(): lax.all_gather(half, 'ep', axis=1, tiled=True)]
    reduce_scatter x1 -> x0, waiting for transfers between devices: 18 us -> none  [body(): lax.psum_scatter(partial, 'tp', scatter_dimension=0, tiled=True)]
    all_to_all x1 -> x0, starting transfers between devices: 9.23 us -> none  [body(): lax.all_to_all(grid.reshape(row_count, owners, local_experts).transpose(1...]
    slice x3 -> x0, local copies, waits for them, and re-layouts: 5.43 us -> none  [the longest x2 4.38 us: attend(): key_heads = both[0].reshape(-1, local_heads, HEAD_DIM)]
    dot_general x3 -> x0, matrix products: 4.07 us -> none  [the longest x1 1.47 us: attend(): jnp.einsum('hqk,khd->hqd', weights.astype(jnp.bfloat16), value_heads, pre...]
  transfers between devices with their start and end apart: 6 -> 1, of which waited for: 6 -> 1; matrix products, arithmetic and copies ran while one was open for 3% -> 0% of each run, Pallas kernels for 0% -> 0%
where the time goes in v2:
time: 225 us; the launch traced here: 223 us
  waiting for transfers between devices  68.9 us (31%)
  Pallas kernels  66.2 us (29%)
  matrix products  57.7 us (26%)
  between operations  13.5 us (6%)
  local copies, waits for them, and re-layouts  6.29 us (3%)
  other arithmetic  6.06 us (3%)
  blocking collectives  4.1 us (2%)
    reduce_scatter x1, waiting for transfers between devices, body(): lax.psum_scatter(owned, ('ep', 'tp'), scatter_dimension=0, tiled=True)  68.9 us
    pallas_call x1, Pallas kernels, front(): pl.pallas_call(functools.partial(front_kernel, count), name='front', out_...  66.2 us
    dot_general x4, matrix products, body(): jnp.dot(hidden.astype(jnp.bfloat16), down_weight[e], preferred_element_ty...  40.3 us
    dot_general x4, matrix products, body(): jnp.dot(normed, gate_weight[e], preferred_element_type=jnp.float32)  16.1 us
  transfers between devices with their start and end apart: 1, of which 1 were waited for; matrix products, arithmetic and copies ran while one was open for 0% of the time, Pallas kernels for 0%

profile of v2, /device:TPU:17, one launch (start us, length us, event | category | flops | bytes accessed | tf_op | source)
XLA Modules:
  0.0 222.7 jit_solution(4716383395060719483)
XLA Ops:
  6.5 0.0 reduce-scatter.2.cloned.1.call-start
  6.5 0.7 iota_compare_fusion.2
  7.3 1.2 dynamic_slice.14
  8.5 0.6 iota_compare_fusion.3
  9.2 0.9 reshape.97
  10.1 0.6 copy.21
  10.7 0.1 concatenate.12
  10.8 0.7 select_reduce_fusion
  11.5 0.6 pad.5
  12.1 66.2 %front.1 = (bf16[384,4096]{1,0:T(8,128)(2,1)}, bf16[128,4096]{1,0:T(8,128)(2,1)}, f32[8,2,16,128]{3,2,1,0:T(8,128)}) custom-call(bf16[64,576]{1,0:T(8,128)(2,1)} %bitcast.107, bf16[64,576]{1,0:T(8,128)(2,1)} %key.1, bf16[64,576]{1,0:T(8,128)(2,1)} %value.1, bf16[4,576,512]{2,1,0:T(8,128)(2,1)} %weight.1, bf16[32,4096]{1,0:T(8,128)(2,1)} %text_ref.1, ...), custom_call_target="tpu_custom_call" | custom-call | tf_op jit(solution)/shard_map/front/pallas_call | solution.py:272
  78.3 0.0 copy-start
  78.4 0.0 copy-start.3
  78.4 5.6 %fusion.3 = f32[384,384]{1,0:T(8,128)} fusion(bf16[384,4096]{1,0:T(8,128)(2,1)} %get-tuple-element.9, bf16[4,4096,384]{2,1,0:T(8,128)(2,1)} %param.21), kind=kOutput, calls=%fused_computation.7 | convolution fusion | flops 1207959552 | bytes 6881280 | tf_op jit(solution)/shard_map/dot_general | solution.py:354
  84.0 0.0 copy-done
  84.0 5.2 %fusion.9 = f32[384,384]{1,0:T(8,128)} fusion(bf16[384,4096]{1,0:T(8,128)(2,1)S(1)} %copy-done, bf16[4,4096,384]{2,1,0:T(8,128)(2,1)} %param.21), kind=kOutput, calls=%fused_computation.13 | convolution fusion | flops 1207959552 | bytes 6881280 | tf_op jit(solution)/shard_map/dot_general | solution.py:354
  89.2 0.0 copy-done.3
  89.2 2.7 %fusion.15 = f32[384,384]{1,0:T(8,128)} fusion(bf16[384,4096]{1,0:T(8,128)(2,1)S(1)} %copy-done, bf16[4,4096,384]{2,1,0:T(8,128)(2,1)S(1)} %copy-done.3), kind=kOutput, calls=%fused_computation.19 | convolution fusion | flops 1207959552 | bytes 6881280 | tf_op jit(solution)/shard_map/dot_general | solution.py:354
  91.9 0.0 copy-start.4
  91.9 2.7 %fusion.21 = f32[384,384]{1,0:T(8,128)} fusion(bf16[384,4096]{1,0:T(8,128)(2,1)S(1)} %copy-done, bf16[4,4096,384]{2,1,0:T(8,128)(2,1)S(1)} %copy-done.3), kind=kOutput, calls=%fused_computation.25 | convolution fusion | flops 1207959552 | bytes 6881280 | tf_op jit(solution)/shard_map/dot_general | solution.py:354
  94.5 0.0 copy-done.4
  94.5 0.2 reduce-window.9
  94.7 0.1 iota_add_fusion
  94.8 0.7 dynamic-slice_bitcast_fusion
  95.5 0.1 reshape.102
  95.6 0.3 convolution_bitcast_fusion
  95.9 9.2 %fusion.17 = f32[384,4096]{1,0:T(8,128)} fusion(bf16[4,384,4096]{2,1,0:T(8,128)(2,1)} %param.23, bf16[384,4096]{1,0:T(8,128)(2,1)S(1)} %copy-done, bf16[4,4096,384]{2,1,0:T(8,128)(2,1)} %param.22, f32[384,384]{1,0:T(8,128)} %fusion.21, f32[384]{0:T(512)S(1)} %get-tuple-element.12), kind=kOutput, calls=%fused_computation.21 | convolution fusion | flops 2416951296 | bytes 16320000 | tf_op jit(solution)/shard_map/dot_general | solution.py:357
  105.1 9.2 %fusion.11 = f32[384,4096]{1,0:T(8,128)} fusion(bf16[4,384,4096]{2,1,0:T(8,128)(2,1)} %param.23, bf16[384,4096]{1,0:T(8,128)(2,1)S(1)} %copy-done, bf16[4,4096,384]{2,1,0:T(8,128)(2,1)} %param.22, f32[384,384]{1,0:T(8,128)} %fusion.15, f32[384]{0:T(512)S(1)} %get-tuple-element.13), kind=kOutput, calls=%fused_computation.15 | convolution fusion | flops 2416951296 | bytes 16320000 | tf_op jit(solution)/shard_map/dot_general | solution.py:357
  114.3 9.1 %fusion.5 = f32[384,4096]{1,0:T(8,128)} fusion(bf16[4,384,4096]{2,1,0:T(8,128)(2,1)} %param.23, bf16[384,4096]{1,0:T(8,128)(2,1)S(1)} %copy-done, bf16[4,4096,384]{2,1,0:T(8,128)(2,1)} %param.22, f32[384,384]{1,0:T(8,128)} %fusion.9, f32[384]{0:T(512)S(1)} %get-tuple-element.14), kind=kOutput, calls=%fused_computation.9 | convolution fusion | flops 2416951296 | bytes 16320000 | tf_op jit(solution)/shard_map/dot_general | solution.py:357
  123.4 12.8 %add_convert_fusion = bf16[384,4096]{1,0:T(8,128)(2,1)S(1)} fusion(f32[384,4096]{1,0:T(8,128)} %fusion.5, f32[384,4096]{1,0:T(8,128)} %fusion.17, f32[384,4096]{1,0:T(8,128)} %fusion.11, bf16[4,384,4096]{2,1,0:T(8,128)(2,1)} %param.23, bf16[384,4096]{1,0:T(8,128)(2,1)} %get-tuple-element.9, bf16[4,4096,384]{2,1,0:T(8,128)(2,1)} %param.22, ...), kind=kOutput, calls=%fused_computation | convolution fusion | flops 2423242752 | bytes 32048640 | tf_op jit(solution)/shard_map/dot_general | solution.py:357
  136.2 0.8 convolution_convert_fusion
  137.0 0.1 slice.93
  137.1 2.4 %pad_maximum_fusion = bf16[8,64,4096]{2,1,0:T(8,128)(2,1)} fusion(bf16[8,32,4096]{2,1,0:T(8,128)(2,1)S(1)} %convolution_convert_fusion, bf16[8,32,4096]{2,1,0:T(8,128)(2,1)S(1)} %bitcast.106), kind=kLoop, calls=%fused_computation.3 | loop fusion | flops 8388608 | bytes 8388608 | tf_op jit(solution)/shard_map/concatenate | solution.py:366
  139.5 0.0 copy-start.1
  139.5 0.0 copy-start.2
  139.6 0.0 reduce-scatter.2.cloned.1.call-update
  139.6 0.1 fusion.106
  139.7 1.0 copy-done.1
  140.8 0.3 convolution_convert_fusion.1
  141.0 68.9 %reduce-scatter.2.cloned.1.call-done = bf16[32,4096]{1,0:T(8,128)(2,1)} async-done(((bf16[512,4096]{1,0:T(8,128)(2,1)}), bf16[32,4096]{1,0:T(8,128)(2,1)}) %reduce-scatter.2.cloned.1.call-update) | async-done | bytes 262160 | tf_op jit(solution)/shard_map/reduce_scatter | solution.py:369
  209.9 0.0 copy-done.2
  209.9 1.1 add_convert_fusion.1
  211.0 4.1 %all_gather.3 = bf16[64,4096]{1,0:T(8,128)(2,1)S(1)} all-gather(bf16[32,4096]{1,0:T(8,128)(2,1)S(1)} %add_convert_fusion.1), channel_id=1, replica_groups=mesh['grp'=2,'ep'=8,'tp'=2] {'tp'}, dimensions={0}, use_global_device_ids=true | all-gather | bytes 786432 | tf_op jit(solution)/shard_map/all_gather | solution.py:377
  215.1 0.8 copy.26
  (4 shorter events, 0.1 us)
Async XLA Ops:
  6.5 203.4 %reduce-scatter.2.cloned.1.call-start = ((), (), s32[]{:S(2)}) async-start(), calls=%async_computation.1 | async-start | bytes 4456448 | tf_op jit(solution)/shard_map/reduce_scatter | solution.py:369
  78.3 5.6 %copy-start = (bf16[384,4096]{1,0:T(8,128)(2,1)S(1)}, bf16[384,4096]{1,0:T(8,128)(2,1)}, u32[]{:S(2)}) copy-start(bf16[384,4096]{1,0:T(8,128)(2,1)} %get-tuple-element.9) | copy-start | bytes 9437188
  78.4 10.8 %copy-start.3 = (bf16[4,4096,384]{2,1,0:T(8,128)(2,1)S(1)}, bf16[4,4096,384]{2,1,0:T(8,128)(2,1)}, u32[]{:S(2)}) copy-start(bf16[4,4096,384]{2,1,0:T(8,128)(2,1)} %param.21) | copy-start | bytes 37748740
  91.9 2.7 %copy-start.4 = (s32[8]{0:T(128)S(1)}, s32[8]{0:T(128)}, u32[]{:S(2)}) copy-start(s32[8]{0:T(128)} %param.16) | copy-start | bytes 100
  139.5 1.2 copy-start.1
  139.5 70.4 %copy-start.2 = (bf16[32,4096]{1,0:T(8,128)(2,1)S(1)}, bf16[32,4096]{1,0:T(8,128)(2,1)}, u32[]{:S(2)}) copy-start(bf16[32,4096]{1,0:T(8,128)(2,1)} %text_ref.1) | copy-start | bytes 786436
Sparse Core Ops, SparseCore 0:
  139.7 70.1 reduce-scatter.1

commit v3 on v2

--- a/solution.py
+++ b/solution.py
@@ -296,6 +296,227 @@
     )(queries, key_rows, value_rows, merger_weight, text_rows, norm_gain.reshape(1, -1), grid)
 
 
+def back_kernel(
+    count,
+    normed, gates, pick, gate_hbm, up_hbm, down_hbm,
+    out_ref,
+    pair_w, down, hidden, acc, pin, cross0, cross1, zin, fin,
+    load_sem, down_sem, pair_send, pair_recv, y_send, y_recv, z_send, z_recv,
+):
+    core, me = lax.axis_index("tp"), lax.axis_index("ep")
+    line = count // 2
+    a, b = me // 2, me % 2
+    experts, width, units = gate_hbm.shape
+    total_rows = normed.shape[0]
+    visual = pick.shape[1]
+    texts = (total_rows - visual) // count
+    slots = pick.shape[0] // count
+    span = acc.shape[4]
+    slot_total = pair_w.shape[0]
+    step_rows = 384 if total_rows % 384 == 0 else total_rows
+
+    def load(e, which):
+        slot = e % slot_total
+        source = (gate_hbm, up_hbm)[which]
+        return pltpu.make_async_copy(
+            source.at[e], pair_w.at[slot, :, pl.ds(which * units, units)], load_sem.at[slot, which]
+        )
+
+    def load_down(e):
+        return pltpu.make_async_copy(
+            down_hbm.at[e], down.at[pl.ds(e * units, units), :], down_sem.at[e]
+        )
+
+    for e in range(slot_total):
+        load(e, 0).start()
+        load(e, 1).start()
+    for e in range(experts):
+        load_down(e).start()
+    greet(count)
+
+    @pl.loop(0, experts)
+    def _(e):
+        load(e, 0).wait()
+        load(e, 1).wait()
+        for first in range(0, total_rows, step_rows):
+            rows = slice(first, first + step_rows)
+            both = jnp.dot(
+                normed[rows, :], pair_w[e % slot_total], preferred_element_type=jnp.float32
+            )
+            value = both[:, :units]
+            gated = value / (1.0 + jnp.exp(-value)) * both[:, units:] * gates[e, rows, :]
+            hidden[rows, pl.ds(pl.multiple_of(e * units, 128), units)] = gated.astype(jnp.bfloat16)
+
+        @pl.when(e + slot_total < experts)
+        def _():
+            load(e + slot_total, 0).start()
+            load(e + slot_total, 1).start()
+
+    for e in range(experts):
+        load_down(e).wait()
+    chunk = 512
+    base = total_rows - visual
+
+    def half_sums(side, half, add):
+        for offset in range(0, span, chunk):
+            start = pl.multiple_of(side * 2 * span + half * span + offset, chunk)
+            weight = down[:, pl.ds(start, chunk)]
+            lanes = slice(offset, offset + chunk)
+            text = jnp.dot(hidden[:base, :], weight, preferred_element_type=jnp.float32)
+            seen = jnp.dot(hidden[base:, :], weight, preferred_element_type=jnp.float32)
+            placed = jnp.dot(
+                pick[...], seen.astype(jnp.bfloat16), preferred_element_type=jnp.float32
+            )
+            for s in range(count):
+                sums = jnp.concatenate(
+                    [text[s * texts : (s + 1) * texts], placed[s * slots : (s + 1) * slots]]
+                )
+                if add:
+                    sums = sums + pin[half, s % 2, s // 2, :, lanes].astype(jnp.float32)
+                acc[half, s % 2, s // 2, :, lanes] = sums.astype(jnp.bfloat16)
+
+    swaps = [
+        to_partner(acc.at[h], pin.at[h], pair_send.at[h], pair_recv.at[h]) for h in range(2)
+    ]
+    for h in range(2):
+        half_sums(1 - core, h, False)
+        swaps[h].start()
+
+    def remote(src, dst, send_sem, recv_sem, target):
+        return pltpu.make_async_remote_copy(
+            src_ref=src, dst_ref=dst, send_sem=send_sem, recv_sem=recv_sem,
+            device_id={"ep": target}, device_id_type=MESH,
+        )
+
+    other = a * 2 + 1 - b
+    swaps[0].wait()
+    half_sums(core, 0, True)
+    first_cross = remote(acc.at[0, 1 - b], cross0, y_send.at[0], y_recv.at[0], other)
+    first_cross.start()
+    swaps[1].wait()
+    half_sums(core, 1, True)
+
+    places = ((0, b), (1, b), (1, 1 - b))
+
+    def hop(q, target, way):
+        half, column = places[q]
+        towards = jnp.clip(a + (1, -1)[way], 0, line - 1) * 2 + b
+        return remote(
+            acc.at[half, column, target], zin.at[q, target + 1 - way],
+            z_send.at[q, target, way], z_recv.at[q, target, way], towards,
+        )
+
+    def take(q, target, way):
+        half, column = places[q]
+        hop(q, target, way).wait_recv()
+        acc[half, column, target] = (
+            acc[half, column, target].astype(jnp.float32)
+            + zin[q, target + 1 - way].astype(jnp.float32)
+        ).astype(jnp.bfloat16)
+
+    def flow(q, i):
+        right, left = line - 1 - i, i
+
+        @pl.when(right > a)
+        def _():
+            @pl.when(a > 0)
+            def _():
+                take(q, right, 0)
+
+            hop(q, right, 0).start()
+
+        @pl.when(left < a)
+        def _():
+            @pl.when(a < line - 1)
+            def _():
+                take(q, left, 1)
+
+            hop(q, left, 1).start()
+
+    def land(q):
+        @pl.when(a > 0)
+        def _():
+            take(q, a, 0)
+
+        @pl.when(a < line - 1)
+        def _():
+            take(q, a, 1)
+
+    flow(2, 0)
+    flow(1, 0)
+    first_cross.wait()
+    for t in range(line):
+        acc[0, b, t] = (
+            acc[0, b, t].astype(jnp.float32) + cross0[t].astype(jnp.float32)
+        ).astype(jnp.bfloat16)
+    flow(0, 0)
+    for i in range(1, line - 1):
+        for q in (2, 1, 0):
+            flow(q, i)
+    land(2)
+    last_cross = remote(acc.at[1, 1 - b, a], cross1, y_send.at[1], y_recv.at[1], other)
+    last_cross.start()
+    land(1)
+    land(0)
+    fin[core, 0] = acc[0, b, a]
+    last_cross.wait()
+    fin[core, 1] = (
+        acc[1, b, a].astype(jnp.float32) + cross1[...].astype(jnp.float32)
+    ).astype(jnp.bfloat16)
+    to_partner(fin.at[core], fin.at[core], pair_send.at[2], pair_recv.at[2]).start()
+    for q in range(3):
+        for t in range(line):
+
+            @pl.when(t > a)
+            def _():
+                hop(q, t, 0).wait_send()
+
+            @pl.when(t < a)
+            def _():
+                hop(q, t, 1).wait_send()
+
+    to_partner(fin.at[core], fin.at[core], pair_send.at[2], pair_recv.at[2]).wait_send()
+    to_partner(fin.at[1 - core], fin.at[1 - core], pair_send.at[2], pair_recv.at[2]).wait_recv()
+    for c in range(2):
+        for h in range(2):
+            out_ref[:, (c * 2 + h) * span : (c * 2 + h + 1) * span] = fin[c, h]
+
+
+def back(normed, gates, pick, gate_weight, up_weight, down_weight):
+    count = lax.axis_size("ep")
+    line = count // 2
+    experts, width, units = gate_weight.shape
+    total_rows = normed.shape[0]
+    owned = (total_rows - pick.shape[1] + pick.shape[0]) // count
+    span = width // 4
+    bf16 = jnp.bfloat16
+    dma = pltpu.SemaphoreType.DMA
+    vmem, hbm = pl.BlockSpec(memory_space=pltpu.VMEM), pl.BlockSpec(memory_space=pl.ANY)
+    return pl.pallas_call(
+        functools.partial(back_kernel, count),
+        name="back",
+        out_shape=jax.ShapeDtypeStruct((owned, width), bf16),
+        in_specs=[vmem] * 3 + [hbm] * 3,
+        out_specs=vmem,
+        scratch_shapes=[
+            pltpu.VMEM((min(2, experts), width, 2 * units), bf16),
+            pltpu.VMEM((experts * units, width), bf16),
+            pltpu.VMEM((total_rows, experts * units), bf16),
+            pltpu.VMEM((2, 2, line, owned, span), bf16),
+            pltpu.VMEM((2, 2, line, owned, span), bf16),
+            pltpu.VMEM((line, owned, span), bf16),
+            pltpu.VMEM((owned, span), bf16),
+            pltpu.VMEM((3, line + 1, owned, span), bf16),
+            pltpu.VMEM((2, 2, owned, span), bf16),
+            dma((2, 2)), dma((experts,)), dma((3,)), dma((3,)), dma((2,)), dma((2,)),
+            dma((3, line, 2)), dma((3, line, 2)),
+        ],
+        compiler_params=pltpu.CompilerParams(
+            collective_id=1, has_side_effects=True, vmem_limit_bytes=62 * MIB
+        ),
+    )(normed, gates, pick, gate_weight, up_weight, down_weight)
+
+
 def body(
     query_rows,
     key_rows,
@@ -349,32 +570,19 @@
     )
     all_grid = jnp.concatenate([text_grid, visual_grid], axis=0)
 
-    total = None
-    for e in range(local_experts):
-        gate_value = jnp.dot(normed, gate_weight[e], preferred_element_type=jnp.float32)
-        up_value = jnp.dot(normed, up_weight[e], preferred_element_type=jnp.float32)
-        hidden = jax.nn.silu(gate_value) * up_value * all_grid[:, e : e + 1]
-        term = jnp.dot(
-            hidden.astype(jnp.bfloat16), down_weight[e], preferred_element_type=jnp.float32
-        )
-        total = term if total is None else total + term
-    total = total.astype(jnp.bfloat16)
-    slot_sum = jnp.einsum(
-        "ojv,vd->ojd", pick.astype(jnp.bfloat16), total[owners * text_count :],
-        preferred_element_type=jnp.float32,
-    ).astype(jnp.bfloat16)
-    owned = jnp.concatenate(
-        [total[: owners * text_count].reshape(owners, text_count, width), slot_sum], axis=1
-    ).reshape(-1, width)
-    combined = lax.psum_scatter(owned, ("ep", "tp"), scatter_dimension=0, tiled=True)
+    combined = back(
+        normed,
+        all_grid.T[:, :, None],
+        pick.reshape(owners * slot_count, visual_total).astype(jnp.bfloat16),
+        gate_weight,
+        up_weight,
+        down_weight,
+    )
     my_visual = jnp.dot(
         pick[owner].astype(jnp.bfloat16), visual, preferred_element_type=jnp.float32
     ).astype(jnp.bfloat16)
     rows = jnp.concatenate([text_rows, my_visual], axis=0)
-    share = row_count // lax.axis_size("tp")
-    residual = lax.dynamic_slice_in_dim(rows, lax.axis_index("tp") * share, share, 0)
-    out = (residual.astype(jnp.float32) + combined.astype(jnp.float32)).astype(jnp.bfloat16)
-    return lax.all_gather(out, "tp", axis=0, tiled=True)
+    return (rows.astype(jnp.float32) + combined.astype(jnp.float32)).astype(jnp.bfloat16)
 
 
 def solution(mesh):

time: 225 us -> 149 us (0.66)
  waiting for transfers between devices: 68.9 us -> 0 us
  Pallas kernels: 66.2 us -> 135 us
  matrix products: 57.7 us -> 1.77 us
  between operations: 13.5 us -> 0.06 us
  blocking collectives: 4.1 us -> 0 us
    reduce_scatter x1 -> x0, waiting for transfers between devices: 68.9 us -> none  [body(): lax.psum_scatter(owned, ('ep', 'tp'), scatter_dimension=0, tiled=True)]
    pallas_call x0 -> x1, Pallas kernels: none -> 68.8 us  [back(): pl.pallas_call(functools.partial(back_kernel, count), name='back', out_sh...]
    dot_general x9 -> x0, matrix products: 57.2 us -> none  [the longest x4 40.3 us: body(): jnp.dot(hidden.astype(jnp.bfloat16), down_weight[e], preferred_element_ty...]
    all_gather x1 -> x0, blocking collectives: 4.1 us -> none  [body(): return lax.all_gather(out, 'tp', axis=0, tiled=True)]
    concatenate x1 -> x0, other arithmetic: 2.42 us -> none  [body(): jnp.concatenate([total[:owners * text_count].reshape(owners, text_count,...]
  transfers between devices with their start and end apart: 1 -> 0, of which waited for: 1 -> 0; matrix products, arithmetic and copies ran while one was open for 0% -> 0% of each run, Pallas kernels for 0% -> 0%
where the time goes in v3:
time: 149 us
  Pallas kernels  135 us (91%)
  other arithmetic  6.53 us (4%)
  local copies, waits for them, and re-layouts  5.66 us (4%)
  matrix products  1.77 us (1%)
    pallas_call x1, Pallas kernels, back(): pl.pallas_call(functools.partial(back_kernel, count), name='back', out_sh...  68.8 us
    pallas_call x1, Pallas kernels, front(): pl.pallas_call(functools.partial(front_kernel, count), name='front', out_...  66.2 us

profile of v3, /device:TPU:17, one launch (start us, length us, event | category | flops | bytes accessed | tf_op | source)
XLA Modules:
  0.0 149.0 jit_solution(17349571255897383913)
XLA Ops:
  0.0 1.2 dynamic_slice.11
  1.2 0.6 iota_compare_fusion.4
  1.9 0.1 concatenate.9
  2.0 0.8 reduce-window.9
  2.8 0.7 bitcast_subtract_fusion
  3.5 0.7 iota_compare_fusion.3
  4.2 0.1 lt.42
  4.3 0.1 iota_add_fusion
  4.3 0.1 add.33
  4.4 0.7 select_reduce_fusion
  5.2 0.6 pad.5
  5.8 0.1 fusion
  5.9 0.8 fusion.3.pick
  6.7 0.9 reshape.102
  7.6 0.6 copy.26
  8.2 66.2 %front.1 = (bf16[384,4096]{1,0:T(8,128)(2,1)}, bf16[128,4096]{1,0:T(8,128)(2,1)}, f32[8,2,16,128]{3,2,1,0:T(8,128)}) custom-call(bf16[64,576]{1,0:T(8,128)(2,1)} %bitcast.28, bf16[64,576]{1,0:T(8,128)(2,1)} %key.1, bf16[64,576]{1,0:T(8,128)(2,1)} %value.1, bf16[4,576,512]{2,1,0:T(8,128)(2,1)} %weight.1, bf16[32,4096]{1,0:T(8,128)(2,1)} %text_ref.1, ...), custom_call_target="tpu_custom_call" | custom-call | tf_op jit(solution)/shard_map/front/pallas_call | solution.py:272
  74.4 1.5 %convolution_convert_fusion = bf16[32,4096]{1,0:T(8,128)(2,1)S(1)} fusion(bf16[128,4096]{1,0:T(8,128)(2,1)} %get-tuple-element.8, pred[8,32,128]{2,1,0:T(32,128)(4,1)S(1)} %fusion, s32[]{:T(128)S(6)} %select_n.10), kind=kOutput, calls=%fused_computation | convolution fusion | flops 33685504 | bytes 1314820 | tf_op jit(solution)/shard_map/dot_general | solution.py:581
  75.9 0.7 dynamic-slice_bitcast_fusion
  76.6 0.3 convolution_bitcast_fusion
  76.9 0.1 reshape.107
  77.0 1.2 copy.28.gates
  78.2 0.0 copy-start
  78.2 68.8 %back.1 = bf16[64,4096]{1,0:T(8,128)(2,1)} custom-call(bf16[384,4096]{1,0:T(8,128)(2,1)} %get-tuple-element.9.normed, f32[4,384,1]{2,1,0:T(8,128)} %copy.28.gates, bf16[256,128]{1,0:T(8,128)(2,1)} %fusion.3.pick, bf16[4,4096,384]{2,1,0:T(8,128)(2,1)} %gate_hbm.1, bf16[4,4096,384]{2,1,0:T(8,128)(2,1)} %up_hbm.1, bf16[4,384,4096]{2,1,0:T(8,128)(2,1)} %down_hbm.1), custom_call_target="tpu_custom_call" | custom-call | tf_op jit(solution)/shard_map/back/pallas_call | solution.py:495
  147.0 0.0 copy-done
  147.0 2.0 %add_convert_fusion = bf16[64,4096]{1,0:T(8,128)(2,1)} fusion(bf16[64,4096]{1,0:T(8,128)(2,1)} %back.1, bf16[32,4096]{1,0:T(8,128)(2,1)S(1)} %convolution_convert_fusion, bf16[32,4096]{1,0:T(8,128)(2,1)S(1)} %copy-done), kind=kLoop, calls=%fused_computation.2 | loop fusion | flops 1835008 | bytes 1572864 | tf_op jit(solution)/shard_map/convert_element_type | solution.py:585
  (3 shorter events, 0.0 us)
Async XLA Ops:
  78.2 68.8 %copy-start = (bf16[32,4096]{1,0:T(8,128)(2,1)S(1)}, bf16[32,4096]{1,0:T(8,128)(2,1)}, u32[]{:S(2)}) copy-start(bf16[32,4096]{1,0:T(8,128)(2,1)} %text_ref.1) | copy-start | bytes 786436

commit v4 on v3

--- a/solution.py
+++ b/solution.py
@@ -162,14 +162,9 @@
     kv_gather.cross()
     for d in range(1, line):
         kv_gather.step(d)
-        if d == 1:
-            grid_gather.start()
-            text_gather.start()
+    text_gather.start()
+    grid_gather.start()
     kv_gather.finish()
-    grid_gather.cross()
-    text_gather.cross()
-    text_gather.step(1)
-    grid_gather.step(1)
 
     patches, features = query.shape
     keys = kv[0].reshape(count * patches, features)
@@ -192,6 +187,8 @@
     for p in range(MERGE):
         att[p // 2, me, p % 2] = attended[p * rows : (p + 1) * rows]
     att_gather.start()
+    text_gather.cross()
+    text_gather.step(1)
     late = [d for d in range(2, line)]
     for d in late[: len(late) // 2]:
         text_gather.step(d)
@@ -200,9 +197,10 @@
         att_gather.step(d)
     for d in late[len(late) // 2 :]:
         text_gather.step(d)
-    for d in late:
+    att_gather.finish()
+    grid_gather.cross()
+    for d in range(1, line):
         grid_gather.step(d)
-    att_gather.finish()
 
     total = None
     for p in range(MERGE):
@@ -226,13 +224,6 @@
     vis_gather.cross()
     for d in range(1, line):
         vis_gather.step(d)
-    grid_gather.finish()
-    for s in range(count):
-        for h in range(2):
-            grid_out[s, h] = grid[h, s]
-    vis_gather.finish()
-    swap_vis = to_partner(vis.at[core], vis.at[core], pair_send.at[2], pair_recv.at[2])
-    swap_vis.start()
     swap_text.wait_send()
     to_partner(text.at[1 - core], text.at[1 - core], pair_send.at[1], pair_recv.at[1]).wait_recv()
     for s in range(count):
@@ -242,6 +233,13 @@
                     s * 2 * mine + c * mine : s * 2 * mine + (c + 1) * mine,
                     h * width // 2 : (h + 1) * width // 2,
                 ] = text[c, h, s]
+    grid_gather.finish()
+    for s in range(count):
+        for h in range(2):
+            grid_out[s, h] = grid[h, s]
+    vis_gather.finish()
+    swap_vis = to_partner(vis.at[core], vis.at[core], pair_send.at[2], pair_recv.at[2])
+    swap_vis.start()
     swap_vis.wait_send()
     to_partner(vis.at[1 - core], vis.at[1 - core], pair_send.at[2], pair_recv.at[2]).wait_recv()
     columns = weight.shape[2]
@@ -442,20 +440,24 @@
         def _():
             take(q, a, 1)
 
-    flow(2, 0)
-    flow(1, 0)
+    for i in range(min(2, line - 1)):
+        flow(2, i)
+        flow(1, i)
     first_cross.wait()
     for t in range(line):
         acc[0, b, t] = (
             acc[0, b, t].astype(jnp.float32) + cross0[t].astype(jnp.float32)
         ).astype(jnp.bfloat16)
     flow(0, 0)
-    for i in range(1, line - 1):
-        for q in (2, 1, 0):
-            flow(q, i)
+    for i in range(2, line - 1):
+        flow(2, i)
+        flow(1, i)
+        flow(0, i - 1)
     land(2)
     last_cross = remote(acc.at[1, 1 - b, a], cross1, y_send.at[1], y_recv.at[1], other)
     last_cross.start()
+    if line > 2:
+        flow(0, line - 2)
     land(1)
     land(0)
     fin[core, 0] = acc[0, b, a]

time: 149 us -> 156 us (1.047); the launches traced: 149 us -> 154 us
  Pallas kernels: 135 us -> 140 us
    pallas_call x1, Pallas kernels: 66.2 us -> 73 us  [front(): pl.pallas_call(functools.partial(front_kernel, count), name='front', out_...]
    pallas_call x1, Pallas kernels: 68.8 us -> 67.1 us  [back(): pl.pallas_call(functools.partial(back_kernel, count), name='back', out_sh...]
where the time goes in v4:
time: 156 us; the launch traced here: 154 us
  Pallas kernels  140 us (90%)
  other arithmetic  6.53 us (4%)
  local copies, waits for them, and re-layouts  5.66 us (4%)
  matrix products  1.77 us (1%)
    pallas_call x1, Pallas kernels, front(): pl.pallas_call(functools.partial(front_kernel, count), name='front', out_...  73 us
    pallas_call x1, Pallas kernels, back(): pl.pallas_call(functools.partial(back_kernel, count), name='back', out_sh...  67.1 us

profile of v4, /device:TPU:17, one launch (start us, length us, event | category | flops | bytes accessed | tf_op | source)
XLA Modules:
  0.0 154.1 jit_solution(2187153597253620894)
XLA Ops:
  0.0 1.2 dynamic_slice.11
  1.2 0.6 iota_compare_fusion.4
  1.9 0.1 concatenate.9
  2.0 0.8 reduce-window.9
  2.8 0.7 bitcast_subtract_fusion
  3.5 0.7 iota_compare_fusion.3
  4.2 0.1 lt.42
  4.3 0.1 iota_add_fusion
  4.3 0.1 add.33
  4.4 0.7 select_reduce_fusion
  5.2 0.6 pad.5
  5.8 0.1 fusion
  5.9 0.8 fusion.3.pick
  6.7 0.9 reshape.102
  7.6 0.6 copy.26
  8.2 73.0 %front.1 = (bf16[384,4096]{1,0:T(8,128)(2,1)}, bf16[128,4096]{1,0:T(8,128)(2,1)}, f32[8,2,16,128]{3,2,1,0:T(8,128)}) custom-call(bf16[64,576]{1,0:T(8,128)(2,1)} %bitcast.28, bf16[64,576]{1,0:T(8,128)(2,1)} %key.1, bf16[64,576]{1,0:T(8,128)(2,1)} %value.1, bf16[4,576,512]{2,1,0:T(8,128)(2,1)} %weight.1, bf16[32,4096]{1,0:T(8,128)(2,1)} %text_ref.1, ...), custom_call_target="tpu_custom_call" | custom-call | tf_op jit(solution)/shard_map/front/pallas_call | solution.py:270
  81.3 1.5 convolution_convert_fusion
  82.8 0.7 dynamic-slice_bitcast_fusion
  83.5 0.3 convolution_bitcast_fusion
  83.8 0.1 reshape.107
  83.9 1.2 copy.28.gates
  85.1 0.0 copy-start
  85.1 67.1 %back.1 = bf16[64,4096]{1,0:T(8,128)(2,1)} custom-call(bf16[384,4096]{1,0:T(8,128)(2,1)} %get-tuple-element.9.normed, f32[4,384,1]{2,1,0:T(8,128)} %copy.28.gates, bf16[256,128]{1,0:T(8,128)(2,1)} %fusion.3.pick, bf16[4,4096,384]{2,1,0:T(8,128)(2,1)} %gate_hbm.1, bf16[4,4096,384]{2,1,0:T(8,128)(2,1)} %up_hbm.1, bf16[4,384,4096]{2,1,0:T(8,128)(2,1)} %down_hbm.1), custom_call_target="tpu_custom_call" | custom-call | tf_op jit(solution)/shard_map/back/pallas_call | solution.py:497
  152.1 0.0 copy-done
  152.1 2.0 %add_convert_fusion = bf16[64,4096]{1,0:T(8,128)(2,1)} fusion(bf16[64,4096]{1,0:T(8,128)(2,1)} %back.1, bf16[32,4096]{1,0:T(8,128)(2,1)S(1)} %convolution_convert_fusion, bf16[32,4096]{1,0:T(8,128)(2,1)S(1)} %copy-done), kind=kLoop, calls=%fused_computation.2 | loop fusion | flops 1835008 | bytes 1572864 | tf_op jit(solution)/shard_map/convert_element_type | solution.py:587
  (3 shorter events, 0.0 us)
Async XLA Ops:
  85.1 67.1 %copy-start = (bf16[32,4096]{1,0:T(8,128)(2,1)S(1)}, bf16[32,4096]{1,0:T(8,128)(2,1)}, u32[]{:S(2)}) copy-start(bf16[32,4096]{1,0:T(8,128)(2,1)} %text_ref.1) | copy-start | bytes 786436
